TPU v7x, 32 devices: a whole 2x2x4 slice. The times are simulated.
32 devices in a mesh: groups: 2 (over x), tlo: 8 (over z, y), thi: 2 (over core).
Axes of the slice: x: 2, y: 2, z: 4, core: 2. Of those that a mesh axis runs over, the one named last changes fastest.
Arguments:
- diagonal_blocks: float32 [32, 512, 512], P(('groups', 'tlo', 'thi')), parts along dimension 0, may hold values from -1 to 8, as said below
- coupling_blocks: float32 [32, 512, 512], P(('groups', 'tlo', 'thi')), parts along dimension 0, may hold values from -3.5 to 0.5
- arrow_blocks: float32 [32, 512, 128], P(('groups', 'tlo', 'thi')), parts along dimension 0, may hold values from -1 to 1
- block_rhs: float32 [32, 512, 256], P(('groups', 'tlo', 'thi')), parts along dimension 0, may hold values from -6 to 6
- tip_block: float32 [256, 128], P('groups'), parts along dimension 0, may hold values from -2 to 26, as said below
- tip_rhs: float32 [256, 256], P('groups'), parts along dimension 0, may hold values from -6 to 6
Outputs:
- chol_factor: float32 [32, 512, 512], P(('groups', 'tlo', 'thi')), parts along dimension 0
- left_factor: float32 [32, 512, 512], P(('groups', 'tlo', 'thi')), parts along dimension 0
- right_factor: float32 [32, 512, 512], P(('groups', 'tlo', 'thi')), parts along dimension 0
- arrow_factor: float32 [32, 512, 128], P(('groups', 'tlo', 'thi')), parts along dimension 0
- forward_rhs: float32 [32, 512, 256], P(('groups', 'tlo', 'thi')), parts along dimension 0
- tip_factor: float32 [256, 128], P('groups'), parts along dimension 0
- tip_solved: float32 [256, 256], P('groups'), parts along dimension 0
- logdet_mean: float32 [2], P('groups'), parts along dimension 0
There are 2 independent parts, one for each index of `groups`. A program takes and returns all parts, laid end to end along the dimension named above; each array names one. Nothing has to cross between parts.
Inputs may be any that keep to these rules, and one draw needn't show every extreme that they name: `diagonal_blocks`: each diagonal block is symmetric; with coupling_blocks, arrow_blocks and tip_block the blocks form a symmetric positive definite matrix. tip_block is symmetric.
All inputs are finite; a program needn't handle non-finite values.
Results may differ from a plain program's by a relative error of at most 0.0003.
Values sent between devices are 32-bit elements; how exact they have to be, the bound alone decides.
A program may use at most 192 MiB of HBM per device.

v0:
```python
import jax
import jax.numpy as jnp
from jax import lax
from jax.sharding import PartitionSpec as P


def shifted(array, axis, by):
    size = lax.axis_size(axis)
    pairs = [(i, i + by) for i in range(size) if 0 <= i + by < size]
    return lax.ppermute(array, axis, pairs)


def product(left_side, right_side):
    return jnp.dot(
        left_side, right_side, precision=lax.Precision.HIGHEST, preferred_element_type=jnp.float32
    )


def lower_solve(factor, right_side):
    return lax.linalg.triangular_solve(factor, right_side, left_side=True, lower=True)


def gated_product(flag, message, start, block_width, skip_start):

    def multiply(values):
        return product(values[:, start : start + block_width].T, values[:, skip_start:])

    def nothing(values):
        return jnp.zeros((block_width, values.shape[1] - skip_start), jnp.float32)

    return lax.cond(flag, multiply, nothing, message)


def pass_along(values, offset):
    return shifted(values, ("tlo", "thi"), offset)


def body(diagonal_blocks, coupling_blocks, arrow_blocks, block_rhs, tip_block, tip_rhs):
    pivot_block = diagonal_blocks[0]
    arrow_block = arrow_blocks[0]
    block_target = block_rhs[0]
    block_width = pivot_block.shape[0]
    tip_width = arrow_block.shape[1]
    probe_count = block_target.shape[1]
    partitions = lax.axis_size(("tlo", "thi"))
    levels = partitions.bit_length() - 1
    half_blocks = partitions // 2
    position = lax.axis_index(("tlo", "thi"))
    ordinal = position + half_blocks
    last_index = partitions - 1
    square_zero = jnp.zeros((block_width, block_width), jnp.float32)
    upper_block = jnp.where(position == last_index, 0.0, coupling_blocks[0])
    lower_block = square_zero
    chol_part = square_zero
    left_part = square_zero
    right_part = square_zero
    arrow_part = jnp.zeros((block_width, tip_width), jnp.float32)
    target_part = jnp.zeros((block_width, probe_count), jnp.float32)
    tip_terms = jnp.zeros((tip_width, tip_width + probe_count), jnp.float32)
    log_terms = jnp.zeros((), jnp.float32)

    def eliminate(operands):
        pivot_now, panel_now = operands
        factor = jnp.linalg.cholesky(pivot_now)
        solved = lower_solve(factor, panel_now)
        tail_part = solved[:, 2 * block_width :]
        tip_piece = product(tail_part[:, :tip_width].T, tail_part)
        log_piece = 2.0 * jnp.sum(jnp.log(jnp.diagonal(factor)))
        return (factor, solved, tip_piece, log_piece)

    def skip_work(operands):
        return (
            square_zero,
            jnp.zeros_like(operands[1]),
            jnp.zeros_like(tip_terms),
            jnp.zeros((), jnp.float32),
        )

    for level_index in range(levels + 1):
        stride = 1 << level_index
        if level_index < levels:
            chosen = (ordinal % stride == 0) & (ordinal // stride % 2 == 1)
        else:
            chosen = position == half_blocks
        between = (ordinal % stride == 0) & (ordinal // stride % 2 == 0)
        takes_left = between & (position + stride <= last_index)
        with_left = level_index + 2 <= levels
        if with_left:
            lower_block = shifted(upper_block, ("tlo", "thi"), stride).T
            left_block = jnp.where(position >= stride, lower_block, 0.0)
        else:
            left_block = square_zero
        panel_now = jnp.concatenate([left_block, upper_block, arrow_block, block_target], axis=1)
        factor, solved, tip_piece, log_piece = lax.cond(
            chosen, eliminate, skip_work, (pivot_block, panel_now)
        )
        chol_part = chol_part + factor
        left_part = left_part + solved[:, :block_width]
        right_part = right_part + solved[:, block_width : 2 * block_width]
        arrow_part = arrow_part + solved[:, 2 * block_width : 2 * block_width + tip_width]
        target_part = target_part + solved[:, 2 * block_width + tip_width :]
        tip_terms = tip_terms + tip_piece
        log_terms = log_terms + log_piece
        if level_index < levels:
            base_column = block_width - block_width
            if with_left:
                left_form = gated_product(chosen, solved, 0, block_width, 0)
            right_form = gated_product(chosen, solved, block_width, block_width, block_width)
            if with_left:
                left_in = pass_along(left_form, -stride)
                pivot_block = pivot_block - jnp.where(takes_left, left_in[:, :block_width], 0.0)
                upper_block = jnp.where(
                    takes_left, -left_in[:, block_width : 2 * block_width], upper_block
                )
                arrow_block = arrow_block - jnp.where(
                    takes_left, left_in[:, 2 * block_width : 2 * block_width + tip_width], 0.0
                )
                block_target = block_target - jnp.where(
                    takes_left, left_in[:, 2 * block_width + tip_width :], 0.0
                )
            right_in = pass_along(right_form, stride)
            pivot_block = pivot_block - jnp.where(
                between, right_in[:, base_column : base_column + block_width], 0.0
            )
            arrow_block = arrow_block - jnp.where(
                between,
                right_in[:, base_column + block_width : base_column + block_width + tip_width],
                0.0,
            )
            block_target = block_target - jnp.where(
                between, right_in[:, base_column + block_width + tip_width :], 0.0
            )
    totals, log_total = lax.psum((tip_terms, log_terms), ("tlo", "thi"))
    reduced = tip_block - totals[:, :tip_width]
    tip_target = tip_rhs - totals[:, tip_width:]
    tip_factor = jnp.linalg.cholesky(reduced)
    tip_solved = lower_solve(tip_factor, tip_target)
    unknowns = partitions * block_width + tip_width
    logdet_mean = (log_total + 2.0 * jnp.sum(jnp.log(jnp.diagonal(tip_factor)))) / unknowns
    return (
        chol_part[None],
        left_part[None],
        right_part[None],
        arrow_part[None],
        target_part[None],
        tip_factor,
        tip_solved,
        logdet_mean.reshape(1),
    )


def solution(mesh):
    in_specs = (
        P(("groups", "tlo", "thi"), None, None),
        P(("groups", "tlo", "thi"), None, None),
        P(("groups", "tlo", "thi"), None, None),
        P(("groups", "tlo", "thi"), None, None),
        P("groups", None),
        P("groups", None),
    )
    out_specs = (
        P(("groups", "tlo", "thi"), None, None),
        P(("groups", "tlo", "thi"), None, None),
        P(("groups", "tlo", "thi"), None, None),
        P(("groups", "tlo", "thi"), None, None),
        P(("groups", "tlo", "thi"), None, None),
        P("groups", None),
        P("groups", None),
        P("groups"),
    )
    return jax.shard_map(body, mesh=mesh, in_specs=in_specs, out_specs=out_specs, check_vma=False)
```

profile of v0, /device:TPU:0, one launch (start us, length us, event | category | flops | bytes accessed | tf_op | source)
XLA Modules:
  0.0 1302.5 jit_solution(9167126219665495119)
XLA Ops:
  16.4 11.0 conditional.12
  32.7 192.6 %collective-permute-start.2 = (f32[512,896]{1,0:T(8,128)}, f32[512,896]{1,0:T(8,128)}, u32[]{:S(2)}, u32[]{:S(2)}) collective-permute-start(f32[512,896]{1,0:T(8,128)} %get-tuple-element.591), channel_id=1, source_target_pairs={{0,1},{1,2},{2,3},{3,4},{4,5},{5,6},{6,7},{7,8},{8,9},{9,10},{10,1... | collective-permute-start | bytes 5505032 | tf_op jit(solution)/shard_map/ppermute | solution.py:10
  231.9 47.0 %collective-permute-start.3 = (f32[512,512]{0,1:T(8,128)}, f32[512,512]{0,1:T(8,128)}, u32[]{:S(2)}, u32[]{:S(2)}) collective-permute-start(f32[512,512]{0,1:T(8,128)} %copy.55), channel_id=1, source_target_pairs={{0,2},{1,3},{2,4},{3,5},{4,6},{5,7},{6,8},{7,9},{8,10},{9,11},{10,... | collective-permute-start | bytes 3145736 | tf_op jit(solution)/shard_map/ppermute | solution.py:10
  281.5 16.5 %collective-permute-done.3 = f32[512,512]{0,1:T(8,128)} collective-permute-done((f32[512,512]{0,1:T(8,128)}, f32[512,512]{0,1:T(8,128)}, u32[]{:S(2)}, u32[]{:S(2)}) %collective-permute-start.3) | collective-permute-done | bytes 1048608 | tf_op jit(solution)/shard_map/ppermute | solution.py:10
  299.9 10.9 conditional.15
  314.8 166.4 %collective-permute-start.5 = (f32[512,896]{1,0:T(8,128)S(1)}, f32[512,896]{1,0:T(8,128)}, u32[]{:S(2)}, u32[]{:S(2)}) collective-permute-start(f32[512,896]{1,0:T(8,128)S(1)} %get-tuple-element.593), channel_id=1, source_target_pairs={{0,2},{1,3},{2,4},{3,5},{4,6},{5,7},{6,8},{7,9},{8,10},{9,11},{10,... | collective-permute-start | bytes 5505032 | tf_op jit(solution)/shard_map/ppermute | solution.py:10
  481.2 44.2 %collective-permute-done.5 = f32[512,896]{1,0:T(8,128)} collective-permute-done((f32[512,896]{1,0:T(8,128)S(1)}, f32[512,896]{1,0:T(8,128)}, u32[]{:S(2)}, u32[]{:S(2)}) %collective-permute-start.5) | collective-permute-done | bytes 1835040 | tf_op jit(solution)/shard_map/ppermute | solution.py:10
  529.3 4.5 collective-permute-start.6
  536.2 9.2 collective-permute-done.6
  547.2 11.2 conditional.18
  562.9 185.2 %collective-permute-start.8 = (f32[512,896]{1,0:T(8,128)}, f32[512,896]{1,0:T(8,128)}, u32[]{:S(2)}, u32[]{:S(2)}) collective-permute-start(f32[512,896]{1,0:T(8,128)} %get-tuple-element.595), channel_id=1, source_target_pairs={{0,4},{1,5},{2,6},{3,7},{4,8},{5,9},{6,10},{7,11},{8,12},{9,13},{1... | collective-permute-start | bytes 5505032 | tf_op jit(solution)/shard_map/ppermute | solution.py:10
  748.2 19.7 %collective-permute-done.8 = f32[512,896]{1,0:T(8,128)} collective-permute-done((f32[512,896]{1,0:T(8,128)}, f32[512,896]{1,0:T(8,128)}, u32[]{:S(2)}, u32[]{:S(2)}) %collective-permute-start.8) | collective-permute-done | bytes 1835040 | tf_op jit(solution)/shard_map/ppermute | solution.py:10
  778.2 175.1 %conditional.21 = (f32[512,512]{1,0:T(8,128)}, f32[512,1408]{1,0:T(8,128)}, f32[]{:T(128)}, f32[128,384]{0,1:T(8,128)S(1)}) conditional(s32[]{:T(128)} %convert_element_type.25, () %tuple.102, (f32[512,512]{1,0:T(8,128)S(1)}, f32[512,1408]{1,0:T(8,128)}) %tuple.105), branch_computations={%region_29.32_spmd, %region_30.34_spmd} | conditional | flops 3478998016 | bytes 51331416 | solution.py:94
  782.4 11.7 cholesky.804
  794.1 9.8 custom-call.70
  808.3 11.7 cholesky.823
  822.6 10.0 custom-call.71
  834.9 11.7 cholesky.844
  848.6 9.8 custom-call.72
  860.7 11.7 cholesky.861
  877.4 11.2 while.13
  888.6 39.3 %custom-call.73 = f32[4,128,128]{1,2,0:T(8,128)S(1)} custom-call(f32[4,128,128]{2,1,0:T(8,128)S(1)} %get-tuple-element.156), custom_call_target="InvertDiagBlocksLowerTriangular" | custom-call | tf_op jit(solution)/shard_map/cond/branch_1_fun/triangular_solve/custom-call.8 | solution.py:20
  943.0 8.7 gather_fusion.1
  954.0 6.6 conditional.22
  954.0 6.6 fusion.15
  967.7 18.3 %collective-permute-done.9 = f32[512,896]{0,1:T(8,128)} collective-permute-done((f32[512,896]{0,1:T(8,128)}, f32[512,896]{0,1:T(8,128)}, u32[]{:S(2)}, u32[]{:S(2)}) %collective-permute-start.9) | collective-permute-done | bytes 1835040 | tf_op jit(solution)/shard_map/ppermute | solution.py:10
  995.1 10.6 conditional.23
  1010.2 8.8 add_bitcast_fusion
  1021.0 186.1 %psum.15 = f32[]{:T(128)} all-reduce(f32[]{:T(128)S(6)} %add.238), channel_id=1, replica_groups=mesh['groups'=2,'tlo'=8,'thi'=2] {'tlo','thi'}, use_global_device_ids=true, to_apply=%region_40.43 | all-reduce | flops 1 | bytes 8 | tf_op jit(solution)/shard_map/psum | solution.py:133
  1207.1 58.3 %all-reduce.3.cloned.1.call-done = f32[128,384]{0,1:T(8,128)} async-done(((f32[128,384]{0,1:T(8,128)}), f32[128,384]{0,1:T(8,128)}) %all-reduce.3.cloned.1.call-update) | async-done | bytes 196624 | tf_op jit(solution)/shard_map/psum | solution.py:133
  1266.4 11.7 cholesky.118
  1281.3 9.8 custom-call.29
  (181 shorter events, 149.5 us)
Async XLA Ops:
  7.2 1258.3 %all-reduce.3.cloned.1.call-start = ((), (), s32[]{:S(2)}) async-start(), calls=%async_computation | async-start | bytes 393216 | tf_op jit(solution)/shard_map/psum | solution.py:133
  7.2 7.7 copy-start.22
  8.6 6.3 copy-start.6
  10.0 4.8 collective-permute-start
  30.0 197.8 %collective-permute-start.1 = (f32[512,1408]{1,0:T(8,128)}, f32[512,1408]{1,0:T(8,128)}, u32[]{:S(2)}, u32[]{:S(2)}) collective-permute-start(f32[512,1408]{1,0:T(8,128)} %get-tuple-element.590), channel_id=1, source_target_pairs={{1,0},{2,1},{3,2},{4,3},{5,4},{6,5},{7,6},{8,7},{9,8},{10,9},{11,1... | collective-permute-start | bytes 8650760 | tf_op jit(solution)/shard_map/ppermute | solution.py:10
  31.2 196.5 %copy-start.5 = (f32[1,512,512]{2,1,0:T(8,128)S(1)}, f32[1,512,512]{2,1,0:T(8,128)}, u32[]{:S(2)}) copy-start(f32[1,512,512]{2,1,0:T(8,128)} %param.33) | copy-start | bytes 3145732
  32.7 195.1 %collective-permute-start.2 = (f32[512,896]{1,0:T(8,128)}, f32[512,896]{1,0:T(8,128)}, u32[]{:S(2)}, u32[]{:S(2)}) collective-permute-start(f32[512,896]{1,0:T(8,128)} %get-tuple-element.591), channel_id=1, source_target_pairs={{0,1},{1,2},{2,3},{3,4},{4,5},{5,6},{6,7},{7,8},{8,9},{9,10},{10,1... | collective-permute-start | bytes 5505032 | tf_op jit(solution)/shard_map/ppermute | solution.py:10
  225.3 53.6 %copy-start.23 = (f32[1,512,128]{2,1,0:T(8,128)S(1)}, f32[1,512,128]{2,1,0:T(8,128)}, u32[]{:S(2)}) copy-start(f32[1,512,128]{2,1,0:T(8,128)} %param.35) | copy-start | bytes 786436
  230.6 67.6 %copy-start = (f32[512,512]{1,0:T(8,128)}, f32[512,512]{1,0:T(8,128)S(1)}, u32[]{:S(2)}) copy-start(f32[512,512]{1,0:T(8,128)S(1)} %get-tuple-element.327) | copy-start | bytes 3145732
  231.9 66.2 %collective-permute-start.3 = (f32[512,512]{0,1:T(8,128)}, f32[512,512]{0,1:T(8,128)}, u32[]{:S(2)}, u32[]{:S(2)}) collective-permute-start(f32[512,512]{0,1:T(8,128)} %copy.55), channel_id=1, source_target_pairs={{0,2},{1,3},{2,4},{3,5},{4,6},{5,7},{6,8},{7,9},{8,10},{9,11},{10,... | collective-permute-start | bytes 3145736 | tf_op jit(solution)/shard_map/ppermute | solution.py:10
  279.9 20.0 %copy-start.19 = (f32[512,128]{1,0:T(8,128)}, f32[512,128]{1,0:T(8,128)S(1)}, u32[]{:S(2)}) copy-start(f32[512,128]{1,0:T(8,128)S(1)} %fusion.209) | copy-start | bytes 786436
  281.5 18.4 %copy-start.13 = (f32[512,256]{1,0:T(8,128)}, f32[512,256]{1,0:T(8,128)S(1)}, u32[]{:S(2)}) copy-start(f32[512,256]{1,0:T(8,128)S(1)} %fusion.203) | copy-start | bytes 1572868
  313.4 212.0 %collective-permute-start.4 = (f32[512,1408]{1,0:T(8,128)}, f32[512,1408]{1,0:T(8,128)}, u32[]{:S(2)}, u32[]{:S(2)}) collective-permute-start(f32[512,1408]{1,0:T(8,128)} %get-tuple-element.592), channel_id=1, source_target_pairs={{2,0},{3,1},{4,2},{5,3},{6,4},{7,5},{8,6},{9,7},{10,8},{11,9},{12,... | collective-permute-start | bytes 8650760 | tf_op jit(solution)/shard_map/ppermute | solution.py:10
  314.8 210.6 %collective-permute-start.5 = (f32[512,896]{1,0:T(8,128)S(1)}, f32[512,896]{1,0:T(8,128)}, u32[]{:S(2)}, u32[]{:S(2)}) collective-permute-start(f32[512,896]{1,0:T(8,128)S(1)} %get-tuple-element.593), channel_id=1, source_target_pairs={{0,2},{1,3},{2,4},{3,5},{4,6},{5,7},{6,8},{7,9},{8,10},{9,11},{10,... | collective-permute-start | bytes 5505032 | tf_op jit(solution)/shard_map/ppermute | solution.py:10
  527.9 6.9 copy-start.14
  529.3 16.1 %collective-permute-start.6 = (f32[512,512]{0,1:T(8,128)}, f32[512,512]{0,1:T(8,128)}, u32[]{:S(2)}, u32[]{:S(2)}) collective-permute-start(f32[512,512]{0,1:T(8,128)} %copy.59), channel_id=1, source_target_pairs={{0,4},{1,5},{2,6},{3,7},{4,8},{5,9},{6,10},{7,11},{8,12},{9,13},{1... | collective-permute-start | bytes 3145736 | tf_op jit(solution)/shard_map/ppermute | solution.py:10
  536.2 11.0 copy-start.11
  560.2 210.8 %collective-permute-start.7 = (f32[512,1408]{1,0:T(8,128)}, f32[512,1408]{1,0:T(8,128)}, u32[]{:S(2)}, u32[]{:S(2)}) collective-permute-start(f32[512,1408]{1,0:T(8,128)} %get-tuple-element.594), channel_id=1, source_target_pairs={{4,0},{5,1},{6,2},{7,3},{8,4},{9,5},{10,6},{11,7},{12,8},{13,9},{1... | collective-permute-start | bytes 8650760 | tf_op jit(solution)/shard_map/ppermute | solution.py:10
  561.5 210.6 %copy-start.12 = (f32[512,256]{1,0:T(8,128)S(1)}, f32[512,256]{1,0:T(8,128)}, u32[]{:S(2)}) copy-start(f32[512,256]{1,0:T(8,128)} %copy-done.11) | copy-start | bytes 1572868
  562.9 205.0 %collective-permute-start.8 = (f32[512,896]{1,0:T(8,128)}, f32[512,896]{1,0:T(8,128)}, u32[]{:S(2)}, u32[]{:S(2)}) collective-permute-start(f32[512,896]{1,0:T(8,128)} %get-tuple-element.595), channel_id=1, source_target_pairs={{0,4},{1,5},{2,6},{3,7},{4,8},{5,9},{6,10},{7,11},{8,12},{9,13},{1... | collective-permute-start | bytes 5505032 | tf_op jit(solution)/shard_map/ppermute | solution.py:10
  772.1 4.3 copy-start.20
  927.9 4.8 copy-start.4
  960.6 5.5 copy-start.33
  960.6 6.3 copy-start.32
  960.6 31.1 %copy-start.21 = (f32[512,128]{1,0:T(8,128)S(1)}, f32[512,128]{1,0:T(8,128)}, u32[]{:S(2)}) copy-start(f32[512,128]{1,0:T(8,128)} %copy-done.20) | copy-start | bytes 786436
  963.5 28.3 %copy-start.10 = (f32[512,256]{1,0:T(8,128)S(1)}, f32[512,256]{1,0:T(8,128)}, u32[]{:S(2)}) copy-start(f32[512,256]{1,0:T(8,128)} %copy-done.9) | copy-start | bytes 1572868
  963.5 22.5 %collective-permute-start.9 = (f32[512,896]{0,1:T(8,128)}, f32[512,896]{0,1:T(8,128)}, u32[]{:S(2)}, u32[]{:S(2)}) collective-permute-start(f32[512,896]{0,1:T(8,128)} %copy.65), channel_id=1, source_target_pairs={{0,8},{1,9},{2,10},{3,11},{4,12},{5,13},{6,14},{7,15},{16,24},{17,... | collective-permute-start | bytes 5505032 | tf_op jit(solution)/shard_map/ppermute | solution.py:10
  995.0 10.6 copy-start.25
  995.0 10.6 copy-start.27
  1010.2 255.3 %copy-start.31 = (f32[128,128]{0,1:T(8,128)S(1)}, f32[128,128]{0,1:T(8,128)}, u32[]{:S(2)}) copy-start(f32[128,128]{0,1:T(8,128)} %copy.75) | copy-start | bytes 196612
  1019.0 273.4 %copy-start.30 = (f32[128,256]{0,1:T(8,128)S(1)}, f32[128,256]{0,1:T(8,128)}, u32[]{:S(2)}) copy-start(f32[128,256]{0,1:T(8,128)} %copy.77) | copy-start | bytes 393220
  1279.4 14.8 %copy-start.8 = (f32[128,128]{1,0:T(8,128)}, f32[128,128]{1,0:T(8,128)S(1)}, u32[]{:S(2)}) copy-start(f32[128,128]{1,0:T(8,128)S(1)} %get-tuple-element.240) | copy-start | bytes 196612
  (6 other events, 7.8 us)
Sparse Core Ops, SparseCore 0:
  1007.6 257.7 all-reduce.2
where the time goes:
time: 1310 us; the launch traced here: 1300 us
  starting transfers between devices  605 us (46%)
  other arithmetic  193 us (15%)
  blocking collectives  186 us (14%)
  waiting for transfers between devices  174 us (13%)
  local copies, waits for them, and re-layouts  62.5 us (5%)
  loops' own time  35 us (3%)
  matrix products  29.5 us (2%)
  between operations  17.1 us (1%)
    ppermute x10, starting transfers between devices, shifted(): return lax.ppermute(array, axis, pairs)  605 us
    psum x1, blocking collectives, body(): totals, log_total = lax.psum((tip_terms, log_terms), ('tlo', 'thi'))  186 us
    ppermute x10, waiting for transfers between devices, shifted(): return lax.ppermute(array, axis, pairs)  116 us
    another operation x14, other arithmetic, eliminate(): factor = jnp.linalg.cholesky(pivot_now)  80.3 us
    psum x1, waiting for transfers between devices, body(): totals, log_total = lax.psum((tip_terms, log_terms), ('tlo', 'thi'))  58.3 us
    another operation x7, other arithmetic, lower_solve(): lax.linalg.triangular_solve(factor, right_side, left_side=True, lower=True)  54.6 us
    another operation x5, loops' own time, body(): lax.cond(chosen, eliminate, skip_work, (pivot_block, panel_now))  34.9 us
  transfers between devices with their start and end apart: 11, of which 9 were waited for; matrix products, arithmetic and copies ran while one was open for 2% of the time, Pallas kernels for 0%

commit v1 on v0

v1 whole, which is shorter than its diff:
```python
import functools

import jax
import jax.numpy as jnp
from jax import lax
from jax.experimental import pallas as pl
from jax.experimental.pallas import tpu as pltpu
from jax.sharding import PartitionSpec as P

TILE = 128
ROWS = 8
PANEL = 4
PRECISE = lax.Precision.HIGHEST


def dot_nn(a, b):
    return lax.dot_general(
        a, b, (((1,), (0,)), ((), ())), precision=PRECISE, preferred_element_type=jnp.float32
    )


def dot_nt(a, b):
    return lax.dot_general(
        a, b, (((1,), (1,)), ((), ())), precision=PRECISE, preferred_element_type=jnp.float32
    )


def dot_tn(a, b):
    return lax.dot_general(
        a, b, (((0,), (0,)), ((), ())), precision=PRECISE, preferred_element_type=jnp.float32
    )


def tile_factor(tile):
    chunks = TILE // ROWS
    row_id = lax.broadcasted_iota(jnp.int32, (TILE, TILE), 0)
    col_id = lax.broadcasted_iota(jnp.int32, (TILE, TILE), 1)
    eye = (row_id == col_id).astype(jnp.float32)
    sub_id = lax.broadcasted_iota(jnp.int32, (ROWS, TILE), 0)
    work = [tile[ROWS * c : ROWS * (c + 1)] for c in range(chunks)]
    back = [eye[ROWS * c : ROWS * (c + 1)] for c in range(chunks)]

    def whole(row):
        return jnp.broadcast_to(row, (ROWS, TILE))

    for first in range(0, TILE, PANEL):
        home, sub = first // ROWS, first % ROWS
        cols = [
            {c: whole(work[c][:, first + k : first + k + 1]) for c in range(home, chunks)}
            for k in range(PANEL)
        ]
        rows = [whole(work[home][sub + k : sub + k + 1]) for k in range(PANEL)]
        backs = [whole(back[home][sub + k : sub + k + 1]) for k in range(PANEL)]
        piv = [[whole(cols[b][home][sub + a : sub + a + 1]) for b in range(PANEL)] for a in range(PANEL)]
        inv = []
        for k in range(PANEL):
            inv.append(1.0 / piv[k][k])
            for a in range(k + 1, PANEL):
                f = piv[a][k] * inv[k]
                rows[a] = rows[a] - f * rows[k]
                backs[a] = backs[a] - f * backs[k]
                for b in range(k + 1, PANEL):
                    piv[a][b] = piv[a][b] - f * piv[k][b]
        for c in range(home, chunks):
            for k in range(PANEL):
                f = cols[k][c] * inv[k]
                if c == home:
                    f = jnp.where(sub_id > sub + k, f, 0.0)
                work[c] = work[c] - f * rows[k]
                back[c] = back[c] - f * backs[k]
                for b in range(k + 1, PANEL):
                    cols[b][c] = cols[b][c] - f * piv[k][b]
    reduced = jnp.concatenate(work, axis=0)
    pivots = jnp.sum(jnp.where(row_id == col_id, reduced, 0.0), axis=1, keepdims=True)
    scale = 1.0 / jnp.sqrt(pivots)
    upper = jnp.where(col_id >= row_id, reduced * scale, 0.0)
    return upper, jnp.concatenate(back, axis=0) * scale


def factor_kernel(s_ref, l_ref, v_ref, a_ref):
    order = s_ref.shape[0]
    a_ref[...] = s_ref[...]

    @pl.loop(0, order // TILE)
    def _(step):
        here = pl.ds(pl.multiple_of(step * TILE, TILE), TILE)
        upper, inverse = tile_factor(a_ref[here, here])
        v_ref[here, :] = inverse
        if order > TILE:
            below = lax.broadcasted_iota(jnp.int32, (order, TILE), 0) >= (step + 1) * TILE
            column = jnp.where(below, dot_nt(a_ref[:, here], inverse), 0.0)
            l_ref[:, here] = column
            a_ref[...] = a_ref[...] - dot_nt(column, column)
        l_ref[here, here] = upper.T


def factor(pivot):
    order = pivot.shape[0]
    return pl.pallas_call(
        factor_kernel,
        out_shape=(
            jax.ShapeDtypeStruct((order, order), jnp.float32),
            jax.ShapeDtypeStruct((order, TILE), jnp.float32),
        ),
        in_specs=[pl.BlockSpec(memory_space=pltpu.VMEM)],
        out_specs=(pl.BlockSpec(memory_space=pltpu.VMEM),) * 2,
        scratch_shapes=[pltpu.VMEM((order, order), jnp.float32)],
        compiler_params=pltpu.CompilerParams(vmem_limit_bytes=32 * 1024 * 1024),
        cost_estimate=pl.CostEstimate(flops=20000000000, bytes_accessed=2 * 4 * order * order, transcendentals=0),
        name="factor",
    )(pivot)


def solve_kernel(count, l_ref, v_ref, *refs):
    order = l_ref.shape[0]
    for src, dst in zip(refs[:count], refs[count:]):
        for k in range(order // TILE):
            at = slice(k * TILE, (k + 1) * TILE)
            part = src[at, :]
            if k > 0:
                part = part - dot_nn(l_ref[at, : k * TILE], dst[: k * TILE, :])
            dst[at, :] = dot_nn(v_ref[at, :], part)


def solve(low, inverse, sides):


    count = len(sides)
    return pl.pallas_call(
        functools.partial(solve_kernel, count),
        out_shape=tuple(jax.ShapeDtypeStruct(s.shape, jnp.float32) for s in sides),
        in_specs=[pl.BlockSpec(memory_space=pltpu.VMEM)] * (2 + count),
        out_specs=(pl.BlockSpec(memory_space=pltpu.VMEM),) * count,
        compiler_params=pltpu.CompilerParams(vmem_limit_bytes=32 * 1024 * 1024),
        cost_estimate=pl.CostEstimate(flops=5000000000, bytes_accessed=8000000, transcendentals=0),
        name="solve",
    )(low, inverse, *sides)


def shifted(array, by):
    size = lax.axis_size(("tlo", "thi"))
    pairs = [(i, i + by) for i in range(size) if 0 <= i + by < size]
    return lax.ppermute(array, ("tlo", "thi"), pairs)


def log_diagonal(matrix):
    row_id = lax.broadcasted_iota(jnp.int32, matrix.shape, 0)
    col_id = lax.broadcasted_iota(jnp.int32, matrix.shape, 1)
    return 2.0 * jnp.sum(jnp.log(jnp.sum(jnp.where(row_id == col_id, matrix, 0.0), axis=1)))


def body(diagonal_blocks, coupling_blocks, arrow_blocks, block_rhs, tip_block, tip_rhs):
    pivot = diagonal_blocks[0]
    arrow = arrow_blocks[0]
    target = block_rhs[0]
    width = pivot.shape[0]
    tip_width = arrow.shape[1]
    partitions = lax.axis_size(("tlo", "thi"))
    levels = partitions.bit_length() - 1
    half = partitions // 2
    position = lax.axis_index(("tlo", "thi"))
    ordinal = position + half
    last = partitions - 1
    upper = jnp.where(position == last, 0.0, coupling_blocks[0])
    lower = jnp.where(position >= 1, shifted(upper, 1).T, 0.0)
    kept = None
    for level in range(levels + 1):
        stride = 1 << level
        final = level == levels
        if final:
            chosen = position == half
        else:
            chosen = (ordinal % stride == 0) & (ordinal // stride % 2 == 1)
        between = (ordinal % stride == 0) & (ordinal // stride % 2 == 0)
        takes_left = between & (position + stride <= last)
        takes_right = between & (position >= stride)
        with_left = level + 2 <= levels
        low, inverse = factor(pivot)
        sides = [arrow, target]
        if not final:
            sides.append(upper)
        if with_left:
            sides.append(lower)
        solved = list(solve(low, inverse, sides))
        m_arrow, m_target = solved[:2]
        zero = jnp.zeros((width, width), jnp.float32)
        m_right = zero if final else solved[2]
        m_left = solved[3] if with_left else zero
        now = (low, m_left, m_right, m_arrow, m_target)
        kept = now if kept is None else tuple(jnp.where(chosen, n, k) for n, k in zip(now, kept))
        if final:
            break
        if with_left:
            from_left = shifted(dot_tn(m_left, m_left), -stride)
        from_right = shifted(dot_tn(m_right, m_right), stride)
        if with_left:
            pivot = pivot - jnp.where(takes_left, from_left, 0.0)
        pivot = pivot - jnp.where(takes_right, from_right, 0.0)
        tail = jnp.concatenate([m_arrow, m_target], axis=1)
        if with_left:
            new_upper = shifted(dot_tn(m_left, m_right), -stride)
            new_lower = shifted(dot_tn(m_right, m_left), stride)
            left_tail = shifted(dot_tn(m_left, tail), -stride)
            arrow = arrow - jnp.where(takes_left, left_tail[:, :tip_width], 0.0)
            target = target - jnp.where(takes_left, left_tail[:, tip_width:], 0.0)
            upper = jnp.where(takes_left, -new_upper, upper)
            lower = jnp.where(takes_right, -new_lower, 0.0)
        right_tail = shifted(dot_tn(m_right, tail), stride)
        arrow = arrow - jnp.where(takes_right, right_tail[:, :tip_width], 0.0)
        target = target - jnp.where(takes_right, right_tail[:, tip_width:], 0.0)
    chol_part, left_part, right_part, arrow_part, target_part = kept
    terms = dot_tn(arrow_part, jnp.concatenate([arrow_part, target_part], axis=1))
    totals, log_total = lax.psum((terms, log_diagonal(chol_part)), ("tlo", "thi"))
    tip_factor, tip_inverse = factor(tip_block - totals[:, :tip_width])
    tip_solved = dot_nn(tip_inverse, tip_rhs - totals[:, tip_width:])
    unknowns = partitions * width + tip_width
    logdet_mean = (log_total + log_diagonal(tip_factor)) / unknowns
    return (
        chol_part[None],
        left_part[None],
        right_part[None],
        arrow_part[None],
        target_part[None],
        tip_factor,
        tip_solved,
        logdet_mean.reshape(1),
    )


def solution(mesh):
    blocks = P(("groups", "tlo", "thi"), None, None)
    tips = P("groups", None)
    return jax.shard_map(
        body,
        mesh=mesh,
        in_specs=(blocks,) * 4 + (tips,) * 2,
        out_specs=(blocks,) * 5 + (tips, tips, P("groups")),
        check_vma=False,
    )
```

time: 1310 us -> 646 us (0.49)
  starting transfers between devices: 605 us -> 97.3 us
  Pallas kernels: 0 us -> 190 us
  other arithmetic: 193 us -> 19.6 us
  blocking collectives: 186 us -> 75.8 us
  local copies, waits for them, and re-layouts: 62.5 us -> 11.4 us
  loops' own time: 35 us -> 0 us
  matrix products: 29.5 us -> 46.1 us
    ppermute x10 -> x20, starting transfers between devices: 605 us -> 97.3 us  [shifted(): return lax.ppermute(array, ('tlo', 'thi'), pairs)]
    pallas_call x0 -> x11, Pallas kernels: none -> 190 us  [the longest x6 155 us: factor(): pl.pallas_call(factor_kernel, out_shape=(jax.ShapeDtypeStruct((order, ord...]
    another operation x24 -> x0, other arithmetic: 147 us -> none  [the longest x14 80.3 us: eliminate(): factor = jnp.linalg.cholesky(pivot_now)]
    psum x1, blocking collectives: 186 us -> 75.8 us  [body(): lax.psum((terms, log_diagonal(chol_part)), ('tlo', 'thi'))]
    dot_general x1 -> x21, matrix products: 6.59 us -> 46.1 us  [the longest x20 45.1 us: dot_tn(): lax.dot_general(a, b, (((0,), (0,)), ((), ())), precision=PRECISE, prefer...]
    another operation x13 -> x0, loops' own time: 35 us -> none  [the longest x5 34.9 us: body(): lax.cond(chosen, eliminate, skip_work, (pivot_block, panel_now))]
    another operation x32 -> x0, local copies, waits for them, and re-layouts: 30.6 us -> none
    another operation x14 -> x0, matrix products: 20.3 us -> none  [the longest x8 12.5 us: lower_solve(): lax.linalg.triangular_solve(factor, right_side, left_side=True, lower=True)]
  transfers between devices with their start and end apart: 11 -> 21, of which waited for: 9 -> 10; matrix products, arithmetic and copies ran while one was open for 2% -> 5% of each run, Pallas kernels for 0% -> 19%
where the time goes in v1:
time: 646 us; the launch traced here: 640 us
  Pallas kernels  190 us (29%)
  waiting for transfers between devices  182 us (28%)
  starting transfers between devices  97.3 us (15%)
  blocking collectives  75.8 us (12%)
  matrix products  46.1 us (7%)
  other arithmetic  19.6 us (3%)
  between operations  18.5 us (3%)
  local copies, waits for them, and re-layouts  11.4 us (2%)
    pallas_call x6, Pallas kernels, factor(): pl.pallas_call(factor_kernel, out_shape=(jax.ShapeDtypeStruct((order, ord...  155 us
    ppermute x20, waiting for transfers between devices, shifted(): return lax.ppermute(array, ('tlo', 'thi'), pairs)  127 us
    ppermute x20, starting transfers between devices, shifted(): return lax.ppermute(array, ('tlo', 'thi'), pairs)  97.3 us
    psum x1, blocking collectives, body(): lax.psum((terms, log_diagonal(chol_part)), ('tlo', 'thi'))  75.8 us
    psum x1, waiting for transfers between devices, body(): lax.psum((terms, log_diagonal(chol_part)), ('tlo', 'thi'))  54.6 us
    dot_general x20, matrix products, dot_tn(): lax.dot_general(a, b, (((0,), (0,)), ((), ())), precision=PRECISE, prefer...  45.1 us
    pallas_call x5, Pallas kernels, solve(): pl.pallas_call(functools.partial(solve_kernel, count), out_shape=tuple((j...  35.3 us
  transfers between devices with their start and end apart: 21, of which 10 were waited for; matrix products, arithmetic and copies ran while one was open for 5% of the time, Pallas kernels for 19%

profile of v1, /device:TPU:0, one launch (start us, length us, event | category | flops | bytes accessed | tf_op | source)
XLA Modules:
  0.0 640.3 jit_solution(9546094777174004898)
XLA Ops:
  9.6 3.4 collective-permute-start
  13.0 29.7 %factor.6 = (f32[512,512]{1,0:T(8,128)S(1)}, f32[512,128]{1,0:T(8,128)S(1)}) custom-call(f32[512,512]{1,0:T(8,128)S(1)} %bitcast.59), custom_call_target="tpu_custom_call" | custom-call | flops 20000000000 | bytes 2097152 | tf_op jit(solution)/shard_map/factor/pallas_call | solution.py:99
  49.5 9.4 %solve.5 = (f32[512,128]{1,0:T(8,128)S(1)}, f32[512,256]{1,0:T(8,128)S(1)}, f32[512,512]{1,0:T(8,128)S(1)}, f32[512,512]{1,0:T(8,128)S(1)}) custom-call(f32[512,512]{1,0:T(8,128)S(1)} %copy-done.35, f32[512,128]{1,0:T(8,128)S(1)} %copy-done.46, f32[512,128]{1,0:T(8,128)S(1)} %bitcast.61, f32[512,256]{1,0:T(8,128)S(1)} %bitcast.60, ...), custom_call_target="tpu_custom_call" | custom-call | flops 5000000000 | bytes 8000000 | tf_op jit(solution)/shard_map/solve/pallas_call | solution.py:129
  66.4 5.0 collective-permute-start.4
  71.5 3.7 collective-permute-start.2
  83.3 3.7 collective-permute-start.6
  88.7 29.7 %factor.7 = (f32[512,512]{1,0:T(8,128)S(1)}, f32[512,128]{1,0:T(8,128)S(1)}) custom-call(f32[512,512]{1,0:T(8,128)S(1)} %select_subtract_fusion.3.s_ref), custom_call_target="tpu_custom_call" | custom-call | flops 20000000000 | bytes 2097152 | tf_op jit(solution)/shard_map/factor/pallas_call | solution.py:99
  119.4 8.2 %solve.6 = (f32[512,128]{1,0:T(8,128)S(1)}, f32[512,256]{1,0:T(8,128)S(1)}, f32[512,512]{1,0:T(8,128)S(1)}, f32[512,512]{1,0:T(8,128)S(1)}) custom-call(f32[512,512]{1,0:T(8,128)S(1)} %get-tuple-element.41.l_ref, f32[512,128]{1,0:T(8,128)S(1)} %get-tuple-element.42.v_ref, f32[512,128]{1,0:T(8,128)S(1)} %fusion.20.refs_0_, f32[512,256]{1,0:T(8,128)S(1)} %fusion.13.refs_1_, ...), custom_call_target="tpu_custom_call" | custom-call | flops 5000000000 | bytes 8000000 | tf_op jit(solution)/shard_map/solve/pallas_call | solution.py:129
  135.1 39.9 %collective-permute-start.10 = (f32[512,384]{1,0:T(8,128)S(1)}, f32[512,384]{1,0:T(8,128)S(1)}, u32[]{:S(2)}, u32[]{:S(2)}) collective-permute-start(f32[512,384]{1,0:T(8,128)S(1)} %fusion.34), channel_id=1, source_target_pairs={{0,2},{1,3},{2,4},{3,5},{4,6},{5,7},{6,8},{7,9},{8,10},{9,11},{10,... | collective-permute-start | bytes 2359304 | tf_op jit(solution)/shard_map/ppermute | solution.py:143
  174.9 4.8 collective-permute-start.8
  188.0 3.4 collective-permute-done.9
  191.4 5.0 collective-permute-start.12
  196.4 54.4 %collective-permute-done.10 = f32[512,384]{1,0:T(8,128)S(1)} collective-permute-done((f32[512,384]{1,0:T(8,128)S(1)}, f32[512,384]{1,0:T(8,128)S(1)}, u32[]{:S(2)}, u32[]{:S(2)}) %collective-permute-start.10) | collective-permute-done | bytes 786464 | tf_op jit(solution)/shard_map/ppermute | solution.py:143
  250.9 22.3 %collective-permute-done.8 = f32[512,512]{1,0:T(8,128)S(1)} collective-permute-done((f32[512,512]{1,0:T(8,128)S(1)}, f32[512,512]{1,0:T(8,128)S(1)}, u32[]{:S(2)}, u32[]{:S(2)}) %collective-permute-start.8) | collective-permute-done | bytes 1048608 | tf_op jit(solution)/shard_map/ppermute | solution.py:143
  273.6 29.7 %factor.8 = (f32[512,512]{1,0:T(8,128)S(1)}, f32[512,128]{1,0:T(8,128)S(1)}) custom-call(f32[512,512]{1,0:T(8,128)S(1)} %select_subtract_fusion.2.s_ref), custom_call_target="tpu_custom_call" | custom-call | flops 20000000000 | bytes 2097152 | tf_op jit(solution)/shard_map/factor/pallas_call | solution.py:99
  304.6 8.2 %solve.7 = (f32[512,128]{1,0:T(8,128)S(1)}, f32[512,256]{1,0:T(8,128)S(1)}, f32[512,512]{1,0:T(8,128)S(1)}, f32[512,512]{1,0:T(8,128)S(1)}) custom-call(f32[512,512]{1,0:T(8,128)S(1)} %get-tuple-element.47.l_ref, f32[512,128]{1,0:T(8,128)S(1)} %get-tuple-element.48.v_ref, f32[512,128]{1,0:T(8,128)S(1)} %fusion.18.refs_0_, f32[512,256]{1,0:T(8,128)S(1)} %fusion.11.refs_1_, ...), custom_call_target="tpu_custom_call" | custom-call | flops 5000000000 | bytes 8000000 | tf_op jit(solution)/shard_map/solve/pallas_call | solution.py:129
  318.6 3.2 fusion.40
  323.0 7.4 %collective-permute-start.16 = (f32[512,384]{1,0:T(8,128)}, f32[512,384]{1,0:T(8,128)}, u32[]{:S(2)}, u32[]{:S(2)}) collective-permute-start(f32[512,384]{1,0:T(8,128)} %fusion.40), channel_id=1, source_target_pairs={{0,4},{1,5},{2,6},{3,7},{4,8},{5,9},{6,10},{7,11},{8,12},{9,13},{1... | collective-permute-start | bytes 2359304 | tf_op jit(solution)/shard_map/ppermute | solution.py:143
  333.3 4.1 collective-permute-start.14
  338.7 3.4 fusion.41
  350.4 16.6 %collective-permute-done.14 = f32[512,512]{1,0:T(8,128)} collective-permute-done((f32[512,512]{1,0:T(8,128)}, f32[512,512]{1,0:T(8,128)}, u32[]{:S(2)}, u32[]{:S(2)}) %collective-permute-start.14) | collective-permute-done | bytes 1048608 | tf_op jit(solution)/shard_map/ppermute | solution.py:143
  370.5 29.5 %factor.9 = (f32[512,512]{1,0:T(8,128)S(1)}, f32[512,128]{1,0:T(8,128)S(1)}) custom-call(f32[512,512]{1,0:T(8,128)S(1)} %select_subtract_fusion.1.s_ref), custom_call_target="tpu_custom_call" | custom-call | flops 20000000000 | bytes 2097152 | tf_op jit(solution)/shard_map/factor/pallas_call | solution.py:99
  401.1 5.9 solve.8
  409.7 6.2 collective-permute-start.19
  416.0 2.9 fusion.42
  422.5 10.8 %collective-permute-done.19 = f32[512,384]{1,0:T(8,128)} collective-permute-done((f32[512,384]{1,0:T(8,128)}, f32[512,384]{1,0:T(8,128)}, u32[]{:S(2)}, u32[]{:S(2)}) %collective-permute-start.19) | collective-permute-done | bytes 786464 | tf_op jit(solution)/shard_map/ppermute | solution.py:143
  435.4 13.4 %collective-permute-done.18 = f32[512,512]{1,0:T(8,128)} collective-permute-done((f32[512,512]{1,0:T(8,128)}, f32[512,512]{1,0:T(8,128)}, u32[]{:S(2)}, u32[]{:S(2)}) %collective-permute-start.18) | collective-permute-done | bytes 1048608 | tf_op jit(solution)/shard_map/ppermute | solution.py:143
  449.0 29.5 %factor.10 = (f32[512,512]{1,0:T(8,128)S(1)}, f32[512,128]{1,0:T(8,128)S(1)}) custom-call(f32[512,512]{1,0:T(8,128)S(1)} %select_subtract_fusion.s_ref), custom_call_target="tpu_custom_call" | custom-call | flops 20000000000 | bytes 2097152 | tf_op jit(solution)/shard_map/factor/pallas_call | solution.py:99
  480.1 3.6 solve.9
  490.4 75.8 %psum.15 = f32[]{:T(128)} all-reduce(f32[]{:T(128)S(6)} %mul.10), channel_id=1, replica_groups=mesh['groups'=2,'tlo'=8,'thi'=2] {'tlo','thi'}, use_global_device_ids=true, to_apply=%region_3.4 | all-reduce | flops 1 | bytes 8 | tf_op jit(solution)/shard_map/psum | solution.py:213
  566.2 54.6 %all-reduce.2.cloned.1.call-done = f32[128,384]{1,0:T(8,128)} async-done(((f32[128,384]{1,0:T(8,128)}), f32[128,384]{1,0:T(8,128)}) %all-reduce.2.cloned.1.call-update) | async-done | bytes 196624 | tf_op jit(solution)/shard_map/psum | solution.py:213
  621.7 6.5 %factor.11 = (f32[128,128]{1,0:T(8,128)}, f32[128,128]{1,0:T(8,128)S(1)}) custom-call(f32[128,128]{1,0:T(8,128)S(1)} %slice_subtract_fusion.2.s_ref), custom_call_target="tpu_custom_call" | custom-call | flops 20000000000 | bytes 131072 | tf_op jit(solution)/shard_map/factor/pallas_call | solution.py:99
  (185 shorter events, 87.9 us)
Async XLA Ops:
  7.2 613.7 %all-reduce.2.cloned.1.call-start = ((), (), s32[]{:S(2)}) async-start(), calls=%async_computation | async-start | bytes 393216 | tf_op jit(solution)/shard_map/psum | solution.py:213
  9.6 33.1 %collective-permute-start = (f32[512,512]{1,0:T(8,128)}, f32[512,512]{1,0:T(8,128)}, u32[]{:S(2)}, u32[]{:S(2)}) collective-permute-start(f32[512,512]{1,0:T(8,128)} %select_bitcast_fusion.3.refs_2_), channel_id=1, source_target_pairs={{0,1},{1,2},{2,3},{3,4},{4,5},{5,6},{6,7},{7,8},{8,9},{9,10},{10,1... | collective-permute-start | bytes 3145736 | tf_op jit(solution)/shard_map/ppermute | solution.py:143
  65.1 18.2 %collective-permute-start.3 = (f32[512,384]{1,0:T(8,128)S(1)}, f32[512,384]{1,0:T(8,128)S(1)}, u32[]{:S(2)}, u32[]{:S(2)}) collective-permute-start(f32[512,384]{1,0:T(8,128)S(1)} %fusion.27), channel_id=1, source_target_pairs={{1,0},{2,1},{3,2},{4,3},{5,4},{6,5},{7,6},{8,7},{9,8},{10,9},{11,1... | collective-permute-start | bytes 2359304 | tf_op jit(solution)/shard_map/ppermute | solution.py:143
  66.4 20.6 %collective-permute-start.4 = (f32[512,384]{1,0:T(8,128)S(1)}, f32[512,384]{1,0:T(8,128)S(1)}, u32[]{:S(2)}, u32[]{:S(2)}) collective-permute-start(f32[512,384]{1,0:T(8,128)S(1)} %fusion.28), channel_id=1, source_target_pairs={{0,1},{1,2},{2,3},{3,4},{4,5},{5,6},{6,7},{7,8},{8,9},{9,10},{10,1... | collective-permute-start | bytes 2359304 | tf_op jit(solution)/shard_map/ppermute | solution.py:143
  71.5 15.7 %collective-permute-start.2 = (f32[512,512]{1,0:T(8,128)S(1)}, f32[512,512]{1,0:T(8,128)S(1)}, u32[]{:S(2)}, u32[]{:S(2)}) collective-permute-start(f32[512,512]{1,0:T(8,128)S(1)} %fusion.26), channel_id=1, source_target_pairs={{0,1},{1,2},{2,3},{3,4},{4,5},{5,6},{6,7},{7,8},{8,9},{9,10},{10,1... | collective-permute-start | bytes 3145736 | tf_op jit(solution)/shard_map/ppermute | solution.py:143
  77.0 10.2 %collective-permute-start.1 = (f32[512,512]{1,0:T(8,128)S(1)}, f32[512,512]{1,0:T(8,128)S(1)}, u32[]{:S(2)}, u32[]{:S(2)}) collective-permute-start(f32[512,512]{1,0:T(8,128)S(1)} %fusion.25), channel_id=1, source_target_pairs={{1,0},{2,1},{3,2},{4,3},{5,4},{6,5},{7,6},{8,7},{9,8},{10,9},{11,1... | collective-permute-start | bytes 3145736 | tf_op jit(solution)/shard_map/ppermute | solution.py:143
  80.2 38.3 %collective-permute-start.5 = (f32[512,512]{1,0:T(8,128)S(1)}, f32[512,512]{1,0:T(8,128)S(1)}, u32[]{:S(2)}, u32[]{:S(2)}) collective-permute-start(f32[512,512]{1,0:T(8,128)S(1)} %fusion.29), channel_id=1, source_target_pairs={{1,0},{2,1},{3,2},{4,3},{5,4},{6,5},{7,6},{8,7},{9,8},{10,9},{11,1... | collective-permute-start | bytes 3145736 | tf_op jit(solution)/shard_map/ppermute | solution.py:143
  83.3 35.4 %collective-permute-start.6 = (f32[512,512]{1,0:T(8,128)S(1)}, f32[512,512]{1,0:T(8,128)S(1)}, u32[]{:S(2)}, u32[]{:S(2)}) collective-permute-start(f32[512,512]{1,0:T(8,128)S(1)} %fusion.30), channel_id=1, source_target_pairs={{0,1},{1,2},{2,3},{3,4},{4,5},{5,6},{6,7},{7,8},{8,9},{9,10},{10,1... | collective-permute-start | bytes 3145736 | tf_op jit(solution)/shard_map/ppermute | solution.py:143
  88.7 29.7 %copy-start.47 = (f32[1,512,512]{2,1,0:T(8,128)S(1)}, f32[1,512,512]{2,1,0:T(8,128)}, u32[]{:S(2)}) copy-start(f32[1,512,512]{2,1,0:T(8,128)} %param.7) | copy-start | bytes 3145732
  127.7 58.4 %copy-start = (f32[512,512]{1,0:T(8,128)}, f32[512,512]{1,0:T(8,128)S(1)}, u32[]{:S(2)}) copy-start(f32[512,512]{1,0:T(8,128)S(1)} %get-tuple-element.45) | copy-start | bytes 3145732
  133.8 57.6 %collective-permute-start.9 = (f32[512,384]{1,0:T(8,128)S(1)}, f32[512,384]{1,0:T(8,128)S(1)}, u32[]{:S(2)}, u32[]{:S(2)}) collective-permute-start(f32[512,384]{1,0:T(8,128)S(1)} %fusion.33), channel_id=1, source_target_pairs={{2,0},{3,1},{4,2},{5,3},{6,4},{7,5},{8,6},{9,7},{10,8},{11,9},{12,... | collective-permute-start | bytes 2359304 | tf_op jit(solution)/shard_map/ppermute | solution.py:143
  135.1 115.7 %collective-permute-start.10 = (f32[512,384]{1,0:T(8,128)S(1)}, f32[512,384]{1,0:T(8,128)S(1)}, u32[]{:S(2)}, u32[]{:S(2)}) collective-permute-start(f32[512,384]{1,0:T(8,128)S(1)} %fusion.34), channel_id=1, source_target_pairs={{0,2},{1,3},{2,4},{3,5},{4,6},{5,7},{6,8},{7,9},{8,10},{9,11},{10,... | collective-permute-start | bytes 2359304 | tf_op jit(solution)/shard_map/ppermute | solution.py:143
  174.9 98.3 %collective-permute-start.8 = (f32[512,512]{1,0:T(8,128)S(1)}, f32[512,512]{1,0:T(8,128)S(1)}, u32[]{:S(2)}, u32[]{:S(2)}) collective-permute-start(f32[512,512]{1,0:T(8,128)S(1)} %fusion.32), channel_id=1, source_target_pairs={{0,2},{1,3},{2,4},{3,5},{4,6},{5,7},{6,8},{7,9},{8,10},{9,11},{10,... | collective-permute-start | bytes 3145736 | tf_op jit(solution)/shard_map/ppermute | solution.py:143
  181.6 91.6 %collective-permute-start.7 = (f32[512,512]{1,0:T(8,128)S(1)}, f32[512,512]{1,0:T(8,128)S(1)}, u32[]{:S(2)}, u32[]{:S(2)}) collective-permute-start(f32[512,512]{1,0:T(8,128)S(1)} %fusion.31), channel_id=1, source_target_pairs={{2,0},{3,1},{4,2},{5,3},{6,4},{7,5},{8,6},{9,7},{10,8},{11,9},{12,... | collective-permute-start | bytes 3145736 | tf_op jit(solution)/shard_map/ppermute | solution.py:143
  184.8 118.5 %collective-permute-start.11 = (f32[512,512]{1,0:T(8,128)S(1)}, f32[512,512]{1,0:T(8,128)S(1)}, u32[]{:S(2)}, u32[]{:S(2)}) collective-permute-start(f32[512,512]{1,0:T(8,128)S(1)} %fusion.35), channel_id=1, source_target_pairs={{2,0},{3,1},{4,2},{5,3},{6,4},{7,5},{8,6},{9,7},{10,8},{11,9},{12,... | collective-permute-start | bytes 3145736 | tf_op jit(solution)/shard_map/ppermute | solution.py:143
  191.4 112.2 %collective-permute-start.12 = (f32[512,512]{1,0:T(8,128)S(1)}, f32[512,512]{1,0:T(8,128)S(1)}, u32[]{:S(2)}, u32[]{:S(2)}) collective-permute-start(f32[512,512]{1,0:T(8,128)S(1)} %fusion.36), channel_id=1, source_target_pairs={{0,2},{1,3},{2,4},{3,5},{4,6},{5,7},{6,8},{7,9},{8,10},{9,11},{10,... | collective-permute-start | bytes 3145736 | tf_op jit(solution)/shard_map/ppermute | solution.py:143
  250.9 52.8 %copy-start.21 = (f32[512,256]{1,0:T(8,128)}, f32[512,256]{1,0:T(8,128)S(1)}, u32[]{:S(2)}) copy-start(f32[512,256]{1,0:T(8,128)S(1)} %fusion.11.refs_1_) | copy-start | bytes 1572868
  273.6 29.7 %copy-start.5 = (f32[512,512]{1,0:T(8,128)}, f32[512,512]{1,0:T(8,128)S(1)}, u32[]{:S(2)}) copy-start(f32[512,512]{1,0:T(8,128)S(1)} %select_subtract_fusion.2.s_ref) | copy-start | bytes 3145732
  321.8 24.7 %collective-permute-start.15 = (f32[512,384]{1,0:T(8,128)}, f32[512,384]{1,0:T(8,128)}, u32[]{:S(2)}, u32[]{:S(2)}) collective-permute-start(f32[512,384]{1,0:T(8,128)} %fusion.39), channel_id=1, source_target_pairs={{4,0},{5,1},{6,2},{7,3},{8,4},{9,5},{10,6},{11,7},{12,8},{13,9},{1... | collective-permute-start | bytes 2359304 | tf_op jit(solution)/shard_map/ppermute | solution.py:143
  323.0 24.8 %collective-permute-start.16 = (f32[512,384]{1,0:T(8,128)}, f32[512,384]{1,0:T(8,128)}, u32[]{:S(2)}, u32[]{:S(2)}) collective-permute-start(f32[512,384]{1,0:T(8,128)} %fusion.40), channel_id=1, source_target_pairs={{0,4},{1,5},{2,6},{3,7},{4,8},{5,9},{6,10},{7,11},{8,12},{9,13},{1... | collective-permute-start | bytes 2359304 | tf_op jit(solution)/shard_map/ppermute | solution.py:143
  333.3 33.7 %collective-permute-start.14 = (f32[512,512]{1,0:T(8,128)}, f32[512,512]{1,0:T(8,128)}, u32[]{:S(2)}, u32[]{:S(2)}) collective-permute-start(f32[512,512]{1,0:T(8,128)} %fusion.38), channel_id=1, source_target_pairs={{0,4},{1,5},{2,6},{3,7},{4,8},{5,9},{6,10},{7,11},{8,12},{9,13},{1... | collective-permute-start | bytes 3145736 | tf_op jit(solution)/shard_map/ppermute | solution.py:143
  337.4 31.5 %collective-permute-start.13 = (f32[512,512]{1,0:T(8,128)}, f32[512,512]{1,0:T(8,128)}, u32[]{:S(2)}, u32[]{:S(2)}) collective-permute-start(f32[512,512]{1,0:T(8,128)} %fusion.37), channel_id=1, source_target_pairs={{4,0},{5,1},{6,2},{7,3},{8,4},{9,5},{10,6},{11,7},{12,8},{13,9},{1... | collective-permute-start | bytes 3145736 | tf_op jit(solution)/shard_map/ppermute | solution.py:143
  342.1 57.9 %collective-permute-start.17 = (f32[512,512]{1,0:T(8,128)S(1)}, f32[512,512]{1,0:T(8,128)S(1)}, u32[]{:S(2)}, u32[]{:S(2)}) collective-permute-start(f32[512,512]{1,0:T(8,128)S(1)} %fusion.41), channel_id=1, source_target_pairs={{4,0},{5,1},{6,2},{7,3},{8,4},{9,5},{10,6},{11,7},{12,8},{13,9},{1... | collective-permute-start | bytes 3145736 | tf_op jit(solution)/shard_map/ppermute | solution.py:143
  349.0 51.3 %copy-start.26 = (f32[512,128]{1,0:T(8,128)}, f32[512,128]{1,0:T(8,128)S(1)}, u32[]{:S(2)}) copy-start(f32[512,128]{1,0:T(8,128)S(1)} %fusion.16.refs_0_) | copy-start | bytes 786436
  350.4 49.9 %copy-start.19 = (f32[512,256]{1,0:T(8,128)}, f32[512,256]{1,0:T(8,128)S(1)}, u32[]{:S(2)}) copy-start(f32[512,256]{1,0:T(8,128)S(1)} %fusion.9.refs_1_) | copy-start | bytes 1572868
  370.5 29.6 %copy-start.10 = (f32[512,512]{1,0:T(8,128)S(1)}, f32[512,512]{1,0:T(8,128)}, u32[]{:S(2)}) copy-start(f32[512,512]{1,0:T(8,128)} %copy-done.9) | copy-start | bytes 3145732
  409.7 23.5 %collective-permute-start.19 = (f32[512,384]{1,0:T(8,128)}, f32[512,384]{1,0:T(8,128)}, u32[]{:S(2)}, u32[]{:S(2)}) collective-permute-start(f32[512,384]{1,0:T(8,128)} %fusion), channel_id=1, source_target_pairs={{0,8},{1,9},{2,10},{3,11},{4,12},{5,13},{6,14},{7,15},{16,24},{17,... | collective-permute-start | bytes 2359304 | tf_op jit(solution)/shard_map/ppermute | solution.py:143
  418.9 29.8 %collective-permute-start.18 = (f32[512,512]{1,0:T(8,128)}, f32[512,512]{1,0:T(8,128)}, u32[]{:S(2)}, u32[]{:S(2)}) collective-permute-start(f32[512,512]{1,0:T(8,128)} %fusion.42), channel_id=1, source_target_pairs={{0,8},{1,9},{2,10},{3,11},{4,12},{5,13},{6,14},{7,15},{16,24},{17,... | collective-permute-start | bytes 3145736 | tf_op jit(solution)/shard_map/ppermute | solution.py:143
  449.0 29.6 %copy-start.36 = (f32[512,512]{1,0:T(8,128)S(1)}, f32[512,512]{1,0:T(8,128)}, u32[]{:S(2)}) copy-start(f32[512,512]{1,0:T(8,128)} %copy-done.34) | copy-start | bytes 3145732
  449.0 29.6 %copy-start.38 = (f32[512,512]{1,0:T(8,128)S(1)}, f32[512,512]{1,0:T(8,128)}, u32[]{:S(2)}) copy-start(f32[512,512]{1,0:T(8,128)} %copy-done.37) | copy-start | bytes 3145732
  449.0 29.6 %copy-start.40 = (f32[512,512]{1,0:T(8,128)S(1)}, f32[512,512]{1,0:T(8,128)}, u32[]{:S(2)}) copy-start(f32[512,512]{1,0:T(8,128)} %copy-done.39) | copy-start | bytes 3145732
  487.7 133.2 %copy-start.52 = (f32[128,128]{1,0:T(8,128)S(1)}, f32[128,128]{1,0:T(8,128)}, u32[]{:S(2)}) copy-start(f32[128,128]{1,0:T(8,128)} %param.10) | copy-start | bytes 196612
  (42 other events, 243.5 us)
Sparse Core Ops, SparseCore 0:
  487.1 133.6 all-reduce.1

commit v2 on v1

--- a/solution.py
+++ b/solution.py
@@ -106,7 +106,7 @@
         out_specs=(pl.BlockSpec(memory_space=pltpu.VMEM),) * 2,
         scratch_shapes=[pltpu.VMEM((order, order), jnp.float32)],
         compiler_params=pltpu.CompilerParams(vmem_limit_bytes=32 * 1024 * 1024),
-        cost_estimate=pl.CostEstimate(flops=20000000000, bytes_accessed=2 * 4 * order * order, transcendentals=0),
+        cost_estimate=pl.CostEstimate(flops=35000000000, bytes_accessed=2 * 4 * order * order, transcendentals=0),
         name="factor",
     )(pivot)
 
@@ -137,10 +137,27 @@
     )(low, inverse, *sides)
 
 
-def shifted(array, by):
+def shifted(array, by, senders):
     size = lax.axis_size(("tlo", "thi"))
-    pairs = [(i, i + by) for i in range(size) if 0 <= i + by < size]
+    pairs = [(i, i + by) for i in senders if 0 <= i + by < size]
     return lax.ppermute(array, ("tlo", "thi"), pairs)
+
+
+def spread(array, root):
+    holders = [root]
+    bit = lax.axis_size(("tlo", "thi")) // 2
+    while bit > 0:
+        others = [i ^ bit for i in holders]
+        array = array + lax.ppermute(array, ("tlo", "thi"), list(zip(holders, others)))
+        holders = holders + others
+        bit //= 2
+    return array
+
+
+def tip_message(chol_part, arrow_part, target_part, here):
+    terms = dot_tn(arrow_part, jnp.concatenate([arrow_part, target_part], axis=1))
+    logs = jnp.broadcast_to(log_diagonal(chol_part), (ROWS, terms.shape[1]))
+    return jnp.where(here, jnp.concatenate([terms, logs], axis=0), 0.0)
 
 
 def log_diagonal(matrix):
@@ -162,18 +179,19 @@
     ordinal = position + half
     last = partitions - 1
     upper = jnp.where(position == last, 0.0, coupling_blocks[0])
-    lower = jnp.where(position >= 1, shifted(upper, 1).T, 0.0)
+    first_level = [i for i in range(partitions) if (i + half) % 2 == 1]
+    lower = shifted(upper, 1, [i - 1 for i in first_level if i >= 1]).T
     kept = None
     for level in range(levels + 1):
         stride = 1 << level
         final = level == levels
+        senders = [i for i in range(partitions) if (i + half) % (2 * stride) == stride]
         if final:
             chosen = position == half
         else:
             chosen = (ordinal % stride == 0) & (ordinal // stride % 2 == 1)
         between = (ordinal % stride == 0) & (ordinal // stride % 2 == 0)
         takes_left = between & (position + stride <= last)
-        takes_right = between & (position >= stride)
         with_left = level + 2 <= levels
         low, inverse = factor(pivot)
         sides = [arrow, target]
@@ -190,27 +208,32 @@
         kept = now if kept is None else tuple(jnp.where(chosen, n, k) for n, k in zip(now, kept))
         if final:
             break
-        if with_left:
-            from_left = shifted(dot_tn(m_left, m_left), -stride)
-        from_right = shifted(dot_tn(m_right, m_right), stride)
-        if with_left:
-            pivot = pivot - jnp.where(takes_left, from_left, 0.0)
-        pivot = pivot - jnp.where(takes_right, from_right, 0.0)
+        if level == levels - 1:
+            early = tip_message(kept[0], kept[3], kept[4], position != half)
+            early = lax.psum(early, ("tlo", "thi"))
+        if with_left:
+            from_left = shifted(dot_tn(m_left, m_left), -stride, senders)
+        from_right = shifted(dot_tn(m_right, m_right), stride, senders)
+        if with_left:
+            pivot = pivot - from_left
+        pivot = pivot - from_right
         tail = jnp.concatenate([m_arrow, m_target], axis=1)
         if with_left:
-            new_upper = shifted(dot_tn(m_left, m_right), -stride)
-            new_lower = shifted(dot_tn(m_right, m_left), stride)
-            left_tail = shifted(dot_tn(m_left, tail), -stride)
-            arrow = arrow - jnp.where(takes_left, left_tail[:, :tip_width], 0.0)
-            target = target - jnp.where(takes_left, left_tail[:, tip_width:], 0.0)
+            new_upper = shifted(dot_tn(m_left, m_right), -stride, senders)
+            new_lower = shifted(dot_tn(m_right, m_left), stride, senders)
+            left_tail = shifted(dot_tn(m_left, tail), -stride, senders)
+            arrow = arrow - left_tail[:, :tip_width]
+            target = target - left_tail[:, tip_width:]
             upper = jnp.where(takes_left, -new_upper, upper)
-            lower = jnp.where(takes_right, -new_lower, 0.0)
-        right_tail = shifted(dot_tn(m_right, tail), stride)
-        arrow = arrow - jnp.where(takes_right, right_tail[:, :tip_width], 0.0)
-        target = target - jnp.where(takes_right, right_tail[:, tip_width:], 0.0)
+            lower = -new_lower
+        right_tail = shifted(dot_tn(m_right, tail), stride, senders)
+        arrow = arrow - right_tail[:, :tip_width]
+        target = target - right_tail[:, tip_width:]
     chol_part, left_part, right_part, arrow_part, target_part = kept
-    terms = dot_tn(arrow_part, jnp.concatenate([arrow_part, target_part], axis=1))
-    totals, log_total = lax.psum((terms, log_diagonal(chol_part)), ("tlo", "thi"))
+    late = tip_message(low, m_arrow, m_target, position == half)
+    totals = early + spread(late, half)
+    log_total = totals[tip_width, 0]
+    totals = totals[:tip_width]
     tip_factor, tip_inverse = factor(tip_block - totals[:, :tip_width])
     tip_solved = dot_nn(tip_inverse, tip_rhs - totals[:, tip_width:])
     unknowns = partitions * width + tip_width

time: 646 us -> 507 us (0.78)
  blocking collectives: 75.8 us -> 0 us
  starting transfers between devices: 97.3 us -> 36.8 us
  waiting for transfers between devices: 182 us -> 171 us
  other arithmetic: 19.6 us -> 27.3 us
    psum x1 -> x0, blocking collectives: 75.8 us -> none  [body(): lax.psum((terms, log_diagonal(chol_part)), ('tlo', 'thi'))]
    ppermute x20, starting transfers between devices: 97.3 us -> 30.7 us  [shifted(): return lax.ppermute(array, ('tlo', 'thi'), pairs)]
    ppermute x20, waiting for transfers between devices: 127 us -> 80.1 us  [shifted(): return lax.ppermute(array, ('tlo', 'thi'), pairs)]
    psum x1, waiting for transfers between devices: 54.6 us -> 80.4 us  [body(): early = lax.psum(early, ('tlo', 'thi'))]
    ppermute x0 -> x4, waiting for transfers between devices: none -> 9.93 us  [spread(): lax.ppermute(array, ('tlo', 'thi'), list(zip(holders, others)))]
    dot_general x20 -> x21, matrix products: 45.1 us -> 44.9 us  [dot_tn(): lax.dot_general(a, b, (((0,), (0,)), ((), ())), precision=PRECISE, prefer...]
  transfers between devices with their start and end apart: 21 -> 25, of which waited for: 10 -> 11; matrix products, arithmetic and copies ran while one was open for 5% -> 7% of each run, Pallas kernels for 19% -> 24%
where the time goes in v2:
time: 507 us; the launch traced here: 501 us
  Pallas kernels  189 us (37%)
  waiting for transfers between devices  171 us (34%)
  matrix products  45.8 us (9%)
  starting transfers between devices  36.8 us (7%)
  other arithmetic  27.3 us (5%)
  between operations  19.2 us (4%)
  local copies, waits for them, and re-layouts  11.6 us (2%)
    pallas_call x6, Pallas kernels, factor(): pl.pallas_call(factor_kernel, out_shape=(jax.ShapeDtypeStruct((order, ord...  155 us
    psum x1, waiting for transfers between devices, body(): early = lax.psum(early, ('tlo', 'thi'))  80.4 us
    ppermute x20, waiting for transfers between devices, shifted(): return lax.ppermute(array, ('tlo', 'thi'), pairs)  80.1 us
    dot_general x21, matrix products, dot_tn(): lax.dot_general(a, b, (((0,), (0,)), ((), ())), precision=PRECISE, prefer...  44.9 us
    pallas_call x5, Pallas kernels, solve(): pl.pallas_call(functools.partial(solve_kernel, count), out_shape=tuple((j...  34.1 us
    ppermute x20, starting transfers between devices, shifted(): return lax.ppermute(array, ('tlo', 'thi'), pairs)  30.7 us
  transfers between devices with their start and end apart: 25, of which 11 were waited for; matrix products, arithmetic and copies ran while one was open for 7% of the time, Pallas kernels for 24%

profile of v2, /device:TPU:0, one launch (start us, length us, event | category | flops | bytes accessed | tf_op | source)
XLA Modules:
  0.0 500.5 jit_solution(6107613813990507207)
XLA Ops:
  8.6 3.4 collective-permute-start
  12.0 29.7 %factor.6 = (f32[512,512]{1,0:T(8,128)S(1)}, f32[512,128]{1,0:T(8,128)S(1)}) custom-call(f32[512,512]{1,0:T(8,128)S(1)} %bitcast.63), custom_call_target="tpu_custom_call" | custom-call | flops 35000000512 | bytes 2097152 | tf_op jit(solution)/shard_map/factor/pallas_call | solution.py:99
  42.5 2.9 copy.14.refs_3_
  49.9 8.2 %solve.5 = (f32[512,128]{1,0:T(8,128)S(1)}, f32[512,256]{1,0:T(8,128)S(1)}, f32[512,512]{1,0:T(8,128)S(1)}, f32[512,512]{1,0:T(8,128)S(1)}) custom-call(f32[512,512]{1,0:T(8,128)S(1)} %copy-done.37, f32[512,128]{1,0:T(8,128)S(1)} %copy-done.48, f32[512,128]{1,0:T(8,128)S(1)} %bitcast.65, f32[512,256]{1,0:T(8,128)S(1)} %bitcast.64, ...), custom_call_target="tpu_custom_call" | custom-call | flops 5000000000 | bytes 8000000 | tf_op jit(solution)/shard_map/solve/pallas_call | solution.py:129
  77.6 29.7 %factor.7 = (f32[512,512]{1,0:T(8,128)S(1)}, f32[512,128]{1,0:T(8,128)S(1)}) custom-call(f32[512,512]{1,0:T(8,128)S(1)} %subtract_subtract_fusion.2.s_ref), custom_call_target="tpu_custom_call" | custom-call | flops 35000000512 | bytes 2097152 | tf_op jit(solution)/shard_map/factor/pallas_call | solution.py:99
  109.2 8.2 %solve.6 = (f32[512,128]{1,0:T(8,128)S(1)}, f32[512,256]{1,0:T(8,128)S(1)}, f32[512,512]{1,0:T(8,128)S(1)}, f32[512,512]{1,0:T(8,128)S(1)}) custom-call(f32[512,512]{1,0:T(8,128)S(1)} %get-tuple-element.41.l_ref, f32[512,128]{1,0:T(8,128)S(1)} %get-tuple-element.42.v_ref, f32[512,128]{1,0:T(8,128)S(1)} %slice_subtract_fusion.12.refs_0_, ...), custom_call_target="tpu_custom_call" | custom-call | flops 5000000000 | bytes 8000000 | tf_op jit(solution)/shard_map/solve/pallas_call | solution.py:129
  134.4 15.5 %collective-permute-done.9 = f32[512,384]{1,0:T(8,128)S(1)} collective-permute-done((f32[512,384]{1,0:T(8,128)S(1)}, f32[512,384]{1,0:T(8,128)S(1)}, u32[]{:S(2)}, u32[]{:S(2)}) %collective-permute-start.9) | collective-permute-done | bytes 786464 | tf_op jit(solution)/shard_map/ppermute | solution.py:143
  150.8 10.8 %collective-permute-done.7 = f32[512,512]{1,0:T(8,128)S(1)} collective-permute-done((f32[512,512]{1,0:T(8,128)S(1)}, f32[512,512]{1,0:T(8,128)S(1)}, u32[]{:S(2)}, u32[]{:S(2)}) %collective-permute-start.7) | collective-permute-done | bytes 1048608 | tf_op jit(solution)/shard_map/ppermute | solution.py:143
  162.0 29.7 %factor.8 = (f32[512,512]{1,0:T(8,128)S(1)}, f32[512,128]{1,0:T(8,128)S(1)}) custom-call(f32[512,512]{1,0:T(8,128)S(1)} %subtract_subtract_fusion.1.s_ref), custom_call_target="tpu_custom_call" | custom-call | flops 35000000512 | bytes 2097152 | tf_op jit(solution)/shard_map/factor/pallas_call | solution.py:99
  192.7 8.2 %solve.7 = (f32[512,128]{1,0:T(8,128)S(1)}, f32[512,256]{1,0:T(8,128)S(1)}, f32[512,512]{1,0:T(8,128)S(1)}, f32[512,512]{1,0:T(8,128)S(1)}) custom-call(f32[512,512]{1,0:T(8,128)S(1)} %get-tuple-element.47.l_ref, f32[512,128]{1,0:T(8,128)S(1)} %get-tuple-element.48.v_ref, f32[512,128]{1,0:T(8,128)S(1)} %slice_subtract_fusion.10.refs_0_, ...), custom_call_target="tpu_custom_call" | custom-call | flops 5000000000 | bytes 8000000 | tf_op jit(solution)/shard_map/solve/pallas_call | solution.py:129
  201.0 2.9 fusion.29
  203.9 2.7 fusion.31
  206.6 3.0 fusion.32
  212.4 2.8 fusion.30
  218.4 3.4 fusion.33
  223.2 32.0 %collective-permute-done.15 = f32[512,384]{1,0:T(8,128)} collective-permute-done((f32[512,384]{1,0:T(8,128)}, f32[512,384]{1,0:T(8,128)}, u32[]{:S(2)}, u32[]{:S(2)}) %collective-permute-start.15) | collective-permute-done | bytes 786464 | tf_op jit(solution)/shard_map/ppermute | solution.py:143
  257.7 11.1 %collective-permute-done.13 = f32[512,512]{1,0:T(8,128)} collective-permute-done((f32[512,512]{1,0:T(8,128)}, f32[512,512]{1,0:T(8,128)}, u32[]{:S(2)}, u32[]{:S(2)}) %collective-permute-start.13) | collective-permute-done | bytes 1048608 | tf_op jit(solution)/shard_map/ppermute | solution.py:143
  270.8 29.9 %factor.9 = (f32[512,512]{1,0:T(8,128)S(1)}, f32[512,128]{1,0:T(8,128)S(1)}) custom-call(f32[512,512]{1,0:T(8,128)S(1)} %subtract_subtract_fusion.s_ref), custom_call_target="tpu_custom_call" | custom-call | flops 35000000512 | bytes 2097152 | tf_op jit(solution)/shard_map/factor/pallas_call | solution.py:99
  301.0 5.9 %solve.8 = (f32[512,128]{1,0:T(8,128)S(1)}, f32[512,256]{1,0:T(8,128)S(1)}, f32[512,512]{1,0:T(8,128)S(1)}) custom-call(f32[512,512]{1,0:T(8,128)S(1)} %get-tuple-element.53.l_ref, f32[512,128]{1,0:T(8,128)S(1)} %get-tuple-element.54.v_ref, f32[512,128]{1,0:T(8,128)S(1)} %slice_subtract_fusion.8.refs_0_, f32[512,256]{1,0:T(8,128)S(1)} %slice_subtract_fusion.1.refs_1_, ...), custom_call_target="tpu_custom_call" | custom-call | flops 5000000000 | bytes 8000000 | tf_op jit(solution)/shard_map/solve/pallas_call | solution.py:129
  306.9 2.9 fusion.34
  309.8 2.7 fusion
  312.5 5.6 %collective-permute-start.19 = (f32[512,384]{1,0:T(8,128)}, f32[512,384]{1,0:T(8,128)}, u32[]{:S(2)}, u32[]{:S(2)}) collective-permute-start(f32[512,384]{1,0:T(8,128)} %fusion), channel_id=1, source_target_pairs={{0,8},{16,24}} | collective-permute-start | bytes 2359304 | tf_op jit(solution)/shard_map/ppermute | solution.py:143
  318.1 2.4 collective-permute-start.18
  324.5 2.5 collective-permute-done.19
  330.6 7.6 %collective-permute-done.18 = f32[512,512]{1,0:T(8,128)} collective-permute-done((f32[512,512]{1,0:T(8,128)}, f32[512,512]{1,0:T(8,128)}, u32[]{:S(2)}, u32[]{:S(2)}) %collective-permute-start.18) | collective-permute-done | bytes 1048608 | tf_op jit(solution)/shard_map/ppermute | solution.py:143
  339.7 29.7 %factor.10 = (f32[512,512]{1,0:T(8,128)S(1)}, f32[512,128]{1,0:T(8,128)S(1)}) custom-call(f32[512,512]{1,0:T(8,128)S(1)} %sub.102.s_ref), custom_call_target="tpu_custom_call" | custom-call | flops 35000000512 | bytes 2097152 | tf_op jit(solution)/shard_map/factor/pallas_call | solution.py:99
  371.9 3.6 solve.9
  378.5 6.3 %collective-permute-done.20 = f32[136,384]{1,0:T(8,128)S(1)} collective-permute-done((f32[136,384]{1,0:T(8,128)S(1)}, f32[136,384]{1,0:T(8,128)S(1)}, u32[]{:S(2)}, u32[]{:S(2)}) %collective-permute-start.20) | collective-permute-done | bytes 208928 | tf_op jit(solution)/shard_map/ppermute | solution.py:151
  387.0 2.5 collective-permute-done.21
  397.2 2.7 select_bitcast_fusion
  400.0 80.4 %all-reduce.4.cloned.1.call-done = f32[136,384]{1,0:T(8,128)} async-done(((f32[136,384]{1,0:T(8,128)}), f32[136,384]{1,0:T(8,128)}) %all-reduce.4.cloned.1.call-update) | async-done | bytes 208912 | tf_op jit(solution)/shard_map/psum | solution.py:213
  482.0 6.5 %factor.11 = (f32[128,128]{1,0:T(8,128)}, f32[128,128]{1,0:T(8,128)S(1)}) custom-call(f32[128,128]{1,0:T(8,128)S(1)} %slice_subtract_fusion.16.s_ref), custom_call_target="tpu_custom_call" | custom-call | flops 35000000512 | bytes 131072 | tf_op jit(solution)/shard_map/factor/pallas_call | solution.py:99
  (201 shorter events, 85.8 us)
Async XLA Ops:
  7.2 473.2 %all-reduce.4.cloned.1.call-start = ((), (), s32[]{:S(2)}) async-start(), calls=%async_computation | async-start | bytes 417792 | tf_op jit(solution)/shard_map/psum | solution.py:213
  8.6 33.8 %collective-permute-start = (f32[512,512]{1,0:T(8,128)S(1)}, f32[512,512]{1,0:T(8,128)}, u32[]{:S(2)}, u32[]{:S(2)}) collective-permute-start(f32[512,512]{1,0:T(8,128)S(1)} %select_bitcast_fusion.3.refs_2_), channel_id=1, source_target_pairs={{0,1},{2,3},{4,5},{6,7},{8,9},{10,11},{12,13},{14,15},{16,17},{18,... | collective-permute-start | bytes 3145736 | tf_op jit(solution)/shard_map/ppermute | solution.py:143
  64.2 10.9 %collective-permute-start.3 = (f32[512,384]{1,0:T(8,128)S(1)}, f32[512,384]{1,0:T(8,128)S(1)}, u32[]{:S(2)}, u32[]{:S(2)}) collective-permute-start(f32[512,384]{1,0:T(8,128)S(1)} %fusion.19), channel_id=1, source_target_pairs={{1,0},{3,2},{5,4},{7,6},{9,8},{11,10},{13,12},{15,14},{17,16},{19,... | collective-permute-start | bytes 2359304 | tf_op jit(solution)/shard_map/ppermute | solution.py:143
  65.5 10.4 %collective-permute-start.4 = (f32[512,384]{1,0:T(8,128)S(1)}, f32[512,384]{1,0:T(8,128)S(1)}, u32[]{:S(2)}, u32[]{:S(2)}) collective-permute-start(f32[512,384]{1,0:T(8,128)S(1)} %fusion.20), channel_id=1, source_target_pairs={{1,2},{3,4},{5,6},{7,8},{9,10},{11,12},{13,14},{17,18},{19,20},{21... | collective-permute-start | bytes 2359304 | tf_op jit(solution)/shard_map/ppermute | solution.py:143
  66.3 9.9 %collective-permute-start.2 = (f32[512,512]{1,0:T(8,128)S(1)}, f32[512,512]{1,0:T(8,128)S(1)}, u32[]{:S(2)}, u32[]{:S(2)}) collective-permute-start(f32[512,512]{1,0:T(8,128)S(1)} %fusion.18), channel_id=1, source_target_pairs={{1,2},{3,4},{5,6},{7,8},{9,10},{11,12},{13,14},{17,18},{19,20},{21... | collective-permute-start | bytes 3145736 | tf_op jit(solution)/shard_map/ppermute | solution.py:143
  68.9 7.8 %collective-permute-start.1 = (f32[512,512]{1,0:T(8,128)S(1)}, f32[512,512]{1,0:T(8,128)S(1)}, u32[]{:S(2)}, u32[]{:S(2)}) collective-permute-start(f32[512,512]{1,0:T(8,128)S(1)} %fusion.17), channel_id=1, source_target_pairs={{1,0},{3,2},{5,4},{7,6},{9,8},{11,10},{13,12},{15,14},{17,16},{19,... | collective-permute-start | bytes 3145736 | tf_op jit(solution)/shard_map/ppermute | solution.py:143
  72.0 35.4 %collective-permute-start.5 = (f32[512,512]{1,0:T(8,128)S(1)}, f32[512,512]{1,0:T(8,128)S(1)}, u32[]{:S(2)}, u32[]{:S(2)}) collective-permute-start(f32[512,512]{1,0:T(8,128)S(1)} %fusion.21), channel_id=1, source_target_pairs={{1,0},{3,2},{5,4},{7,6},{9,8},{11,10},{13,12},{15,14},{17,16},{19,... | collective-permute-start | bytes 3145736 | tf_op jit(solution)/shard_map/ppermute | solution.py:143
  75.2 32.1 %collective-permute-start.6 = (f32[512,512]{1,0:T(8,128)S(1)}, f32[512,512]{1,0:T(8,128)S(1)}, u32[]{:S(2)}, u32[]{:S(2)}) collective-permute-start(f32[512,512]{1,0:T(8,128)S(1)} %fusion.22), channel_id=1, source_target_pairs={{1,2},{3,4},{5,6},{7,8},{9,10},{11,12},{13,14},{17,18},{19,20},{21... | collective-permute-start | bytes 3145736 | tf_op jit(solution)/shard_map/ppermute | solution.py:143
  123.5 26.5 %collective-permute-start.9 = (f32[512,384]{1,0:T(8,128)S(1)}, f32[512,384]{1,0:T(8,128)S(1)}, u32[]{:S(2)}, u32[]{:S(2)}) collective-permute-start(f32[512,384]{1,0:T(8,128)S(1)} %fusion.25), channel_id=1, source_target_pairs={{2,0},{6,4},{10,8},{14,12},{18,16},{22,20},{26,24},{30,28}} | collective-permute-start | bytes 2359304 | tf_op jit(solution)/shard_map/ppermute | solution.py:143
  124.8 25.9 %collective-permute-start.10 = (f32[512,384]{1,0:T(8,128)S(1)}, f32[512,384]{1,0:T(8,128)S(1)}, u32[]{:S(2)}, u32[]{:S(2)}) collective-permute-start(f32[512,384]{1,0:T(8,128)S(1)} %fusion.26), channel_id=1, source_target_pairs={{2,4},{6,8},{10,12},{18,20},{22,24},{26,28}} | collective-permute-start | bytes 2359304 | tf_op jit(solution)/shard_map/ppermute | solution.py:143
  125.5 25.3 %collective-permute-start.8 = (f32[512,512]{1,0:T(8,128)S(1)}, f32[512,512]{1,0:T(8,128)S(1)}, u32[]{:S(2)}, u32[]{:S(2)}) collective-permute-start(f32[512,512]{1,0:T(8,128)S(1)} %fusion.24), channel_id=1, source_target_pairs={{2,4},{6,8},{10,12},{18,20},{22,24},{26,28}} | collective-permute-start | bytes 3145736 | tf_op jit(solution)/shard_map/ppermute | solution.py:143
  128.1 33.6 %collective-permute-start.7 = (f32[512,512]{1,0:T(8,128)S(1)}, f32[512,512]{1,0:T(8,128)S(1)}, u32[]{:S(2)}, u32[]{:S(2)}) collective-permute-start(f32[512,512]{1,0:T(8,128)S(1)} %fusion.23), channel_id=1, source_target_pairs={{2,0},{6,4},{10,8},{14,12},{18,16},{22,20},{26,24},{30,28}} | collective-permute-start | bytes 3145736 | tf_op jit(solution)/shard_map/ppermute | solution.py:143
  131.2 60.6 %collective-permute-start.11 = (f32[512,512]{1,0:T(8,128)S(1)}, f32[512,512]{1,0:T(8,128)S(1)}, u32[]{:S(2)}, u32[]{:S(2)}) collective-permute-start(f32[512,512]{1,0:T(8,128)S(1)} %fusion.27), channel_id=1, source_target_pairs={{2,0},{6,4},{10,8},{14,12},{18,16},{22,20},{26,24},{30,28}} | collective-permute-start | bytes 3145736 | tf_op jit(solution)/shard_map/ppermute | solution.py:143
  149.9 41.8 %collective-permute-start.12 = (f32[512,512]{1,0:T(8,128)S(1)}, f32[512,512]{1,0:T(8,128)S(1)}, u32[]{:S(2)}, u32[]{:S(2)}) collective-permute-start(f32[512,512]{1,0:T(8,128)S(1)} %fusion.28), channel_id=1, source_target_pairs={{2,4},{6,8},{10,12},{18,20},{22,24},{26,28}} | collective-permute-start | bytes 3145736 | tf_op jit(solution)/shard_map/ppermute | solution.py:143
  150.8 41.3 %copy-start.23 = (f32[512,256]{1,0:T(8,128)}, f32[512,256]{1,0:T(8,128)S(1)}, u32[]{:S(2)}) copy-start(f32[512,256]{1,0:T(8,128)S(1)} %slice_subtract_fusion.3.refs_1_) | copy-start | bytes 1572868
  209.6 45.6 %collective-permute-start.15 = (f32[512,384]{1,0:T(8,128)}, f32[512,384]{1,0:T(8,128)}, u32[]{:S(2)}, u32[]{:S(2)}) collective-permute-start(f32[512,384]{1,0:T(8,128)} %fusion.31), channel_id=1, source_target_pairs={{4,0},{12,8},{20,16},{28,24}} | collective-permute-start | bytes 2359304 | tf_op jit(solution)/shard_map/ppermute | solution.py:143
  210.9 44.3 %collective-permute-start.16 = (f32[512,384]{1,0:T(8,128)}, f32[512,384]{1,0:T(8,128)}, u32[]{:S(2)}, u32[]{:S(2)}) collective-permute-start(f32[512,384]{1,0:T(8,128)} %fusion.32), channel_id=1, source_target_pairs={{4,8},{20,24}} | collective-permute-start | bytes 2359304 | tf_op jit(solution)/shard_map/ppermute | solution.py:143
  215.3 42.4 %collective-permute-start.14 = (f32[512,512]{1,0:T(8,128)}, f32[512,512]{1,0:T(8,128)}, u32[]{:S(2)}, u32[]{:S(2)}) collective-permute-start(f32[512,512]{1,0:T(8,128)} %fusion.30), channel_id=1, source_target_pairs={{4,8},{20,24}} | collective-permute-start | bytes 3145736 | tf_op jit(solution)/shard_map/ppermute | solution.py:143
  217.0 51.8 %collective-permute-start.13 = (f32[512,512]{1,0:T(8,128)}, f32[512,512]{1,0:T(8,128)}, u32[]{:S(2)}, u32[]{:S(2)}) collective-permute-start(f32[512,512]{1,0:T(8,128)} %fusion.29), channel_id=1, source_target_pairs={{4,0},{12,8},{20,16},{28,24}} | collective-permute-start | bytes 3145736 | tf_op jit(solution)/shard_map/ppermute | solution.py:143
  221.8 34.5 %copy-start.24 = (f32[512,256]{1,0:T(8,128)S(1)}, f32[512,256]{1,0:T(8,128)}, u32[]{:S(2)}) copy-start(f32[512,256]{1,0:T(8,128)} %copy-done.23) | copy-start | bytes 1572868
  221.8 78.9 %collective-permute-start.17 = (f32[512,512]{1,0:T(8,128)S(1)}, f32[512,512]{1,0:T(8,128)S(1)}, u32[]{:S(2)}, u32[]{:S(2)}) collective-permute-start(f32[512,512]{1,0:T(8,128)S(1)} %fusion.33), channel_id=1, source_target_pairs={{4,0},{12,8},{20,16},{28,24}} | collective-permute-start | bytes 3145736 | tf_op jit(solution)/shard_map/ppermute | solution.py:143
  256.3 44.7 %copy-start.26 = (f32[512,128]{1,0:T(8,128)}, f32[512,128]{1,0:T(8,128)S(1)}, u32[]{:S(2)}) copy-start(f32[512,128]{1,0:T(8,128)S(1)} %slice_subtract_fusion.8.refs_0_) | copy-start | bytes 786436
  257.7 43.2 %copy-start.21 = (f32[512,256]{1,0:T(8,128)}, f32[512,256]{1,0:T(8,128)S(1)}, u32[]{:S(2)}) copy-start(f32[512,256]{1,0:T(8,128)S(1)} %slice_subtract_fusion.1.refs_1_) | copy-start | bytes 1572868
  270.7 29.9 %copy-start.9 = (f32[512,512]{1,0:T(8,128)}, f32[512,512]{1,0:T(8,128)S(1)}, u32[]{:S(2)}) copy-start(f32[512,512]{1,0:T(8,128)S(1)} %subtract_subtract_fusion.s_ref) | copy-start | bytes 3145732
  270.7 29.9 %copy-start.8 = (f32[512,512]{1,0:T(8,128)S(1)}, f32[512,512]{1,0:T(8,128)}, u32[]{:S(2)}) copy-start(f32[512,512]{1,0:T(8,128)} %copy-done.7) | copy-start | bytes 3145732
  312.5 14.5 %collective-permute-start.19 = (f32[512,384]{1,0:T(8,128)}, f32[512,384]{1,0:T(8,128)}, u32[]{:S(2)}, u32[]{:S(2)}) collective-permute-start(f32[512,384]{1,0:T(8,128)} %fusion), channel_id=1, source_target_pairs={{0,8},{16,24}} | collective-permute-start | bytes 2359304 | tf_op jit(solution)/shard_map/ppermute | solution.py:143
  318.1 20.1 %collective-permute-start.18 = (f32[512,512]{1,0:T(8,128)}, f32[512,512]{1,0:T(8,128)}, u32[]{:S(2)}, u32[]{:S(2)}) collective-permute-start(f32[512,512]{1,0:T(8,128)} %fusion.34), channel_id=1, source_target_pairs={{0,8},{16,24}} | collective-permute-start | bytes 3145736 | tf_op jit(solution)/shard_map/ppermute | solution.py:143
  376.2 8.6 %collective-permute-start.20 = (f32[136,384]{1,0:T(8,128)S(1)}, f32[136,384]{1,0:T(8,128)S(1)}, u32[]{:S(2)}, u32[]{:S(2)}) collective-permute-start(f32[136,384]{1,0:T(8,128)S(1)} %pad_select_fusion), channel_id=1, source_target_pairs={{8,0},{24,16}} | collective-permute-start | bytes 626696 | tf_op jit(solution)/shard_map/ppermute | solution.py:151
  384.8 4.6 collective-permute-start.21
  389.5 4.6 collective-permute-start.22
  395.7 84.7 %collective-permute-start.23 = (f32[136,384]{1,0:T(8,128)}, f32[136,384]{1,0:T(8,128)S(1)}, u32[]{:S(2)}, u32[]{:S(2)}) collective-permute-start(f32[136,384]{1,0:T(8,128)} %add.83), channel_id=1, source_target_pairs={{8,9},{0,1},{12,13},{4,5},{10,11},{2,3},{14,15},{6,7},{24,25},{16,... | collective-permute-start | bytes 626696 | tf_op jit(solution)/shard_map/ppermute | solution.py:151
  399.9 82.0 %copy-start.52 = (f32[128,128]{1,0:T(8,128)S(1)}, f32[128,128]{1,0:T(8,128)}, u32[]{:S(2)}) copy-start(f32[128,128]{1,0:T(8,128)} %param.10) | copy-start | bytes 196612
  (46 other events, 279.0 us)
Sparse Core Ops, SparseCore 0:
  393.0 87.3 all-reduce.3

commit v3 on v2

--- a/solution.py
+++ b/solution.py
@@ -154,10 +154,10 @@
     return array
 
 
-def tip_message(chol_part, arrow_part, target_part, here):
+def tip_message(chol_part, arrow_part, target_part):
     terms = dot_tn(arrow_part, jnp.concatenate([arrow_part, target_part], axis=1))
     logs = jnp.broadcast_to(log_diagonal(chol_part), (ROWS, terms.shape[1]))
-    return jnp.where(here, jnp.concatenate([terms, logs], axis=0), 0.0)
+    return jnp.concatenate([terms, logs], axis=0)
 
 
 def log_diagonal(matrix):
@@ -182,6 +182,7 @@
     first_level = [i for i in range(partitions) if (i + half) % 2 == 1]
     lower = shifted(upper, 1, [i - 1 for i in first_level if i >= 1]).T
     kept = None
+    gathered = jnp.zeros((tip_width + ROWS, tip_width + target.shape[1]), jnp.float32)
     for level in range(levels + 1):
         stride = 1 << level
         final = level == levels
@@ -208,9 +209,6 @@
         kept = now if kept is None else tuple(jnp.where(chosen, n, k) for n, k in zip(now, kept))
         if final:
             break
-        if level == levels - 1:
-            early = tip_message(kept[0], kept[3], kept[4], position != half)
-            early = lax.psum(early, ("tlo", "thi"))
         if with_left:
             from_left = shifted(dot_tn(m_left, m_left), -stride, senders)
         from_right = shifted(dot_tn(m_right, m_right), stride, senders)
@@ -218,20 +216,34 @@
             pivot = pivot - from_left
         pivot = pivot - from_right
         tail = jnp.concatenate([m_arrow, m_target], axis=1)
-        if with_left:
-            new_upper = shifted(dot_tn(m_left, m_right), -stride, senders)
-            new_lower = shifted(dot_tn(m_right, m_left), stride, senders)
-            left_tail = shifted(dot_tn(m_left, tail), -stride, senders)
+        message = gathered + tip_message(low, m_arrow, m_target)
+        if with_left:
+            pivot, to_upper, to_lower, to_left, to_right, message = lax.optimization_barrier(
+                (
+                    pivot,
+                    dot_tn(m_left, m_right),
+                    dot_tn(m_right, m_left),
+                    dot_tn(m_left, tail),
+                    dot_tn(m_right, tail),
+                    message,
+                )
+            )
+            upper = jnp.where(takes_left, -shifted(to_upper, -stride, senders), upper)
+            lower = -shifted(to_lower, stride, senders)
+            left_tail = shifted(to_left, -stride, senders)
             arrow = arrow - left_tail[:, :tip_width]
             target = target - left_tail[:, tip_width:]
-            upper = jnp.where(takes_left, -new_upper, upper)
-            lower = -new_lower
-        right_tail = shifted(dot_tn(m_right, tail), stride, senders)
+        else:
+            pivot, to_right, message = lax.optimization_barrier(
+                (pivot, dot_tn(m_right, tail), message)
+            )
+        right_tail = shifted(to_right, stride, senders)
         arrow = arrow - right_tail[:, :tip_width]
         target = target - right_tail[:, tip_width:]
+        gathered = gathered + shifted(message, -stride if with_left else stride, senders)
     chol_part, left_part, right_part, arrow_part, target_part = kept
-    late = tip_message(low, m_arrow, m_target, position == half)
-    totals = early + spread(late, half)
+    totals = gathered + tip_message(low, m_arrow, m_target)
+    totals = spread(jnp.where(position == half, totals, 0.0), half)
     log_total = totals[tip_width, 0]
     totals = totals[:tip_width]
     tip_factor, tip_inverse = factor(tip_block - totals[:, :tip_width])

time: 507 us -> 393 us (0.78)
  waiting for transfers between devices: 171 us -> 47 us
  between operations: 19.2 us -> 8.01 us
  starting transfers between devices: 36.8 us -> 46.2 us
  other arithmetic: 27.3 us -> 33.8 us
    psum x1 -> x0, waiting for transfers between devices: 80.4 us -> none  [body(): early = lax.psum(early, ('tlo', 'thi'))]
    ppermute x20 -> x24, waiting for transfers between devices: 80.1 us -> 37.1 us  [shifted(): return lax.ppermute(array, ('tlo', 'thi'), pairs)]
    ppermute x20 -> x24, starting transfers between devices: 30.7 us -> 40.8 us  [shifted(): return lax.ppermute(array, ('tlo', 'thi'), pairs)]
    unnamed x109 -> x140, local copies, waits for them, and re-layouts: 8.06 us -> 11.9 us
    dot_general x21 -> x24, matrix products: 44.9 us -> 46.6 us  [dot_tn(): lax.dot_general(a, b, (((0,), (0,)), ((), ())), precision=PRECISE, prefer...]
  transfers between devices with their start and end apart: 25 -> 28, of which waited for: 11 -> 6; matrix products, arithmetic and copies ran while one was open for 7% -> 18% of each run, Pallas kernels for 24% -> 45%
where the time goes in v3:
time: 393 us; the launch traced here: 386 us
  Pallas kernels  189 us (48%)
  matrix products  47.5 us (12%)
  waiting for transfers between devices  47 us (12%)
  starting transfers between devices  46.2 us (12%)
  other arithmetic  33.8 us (9%)
  local copies, waits for them, and re-layouts  14.9 us (4%)
  between operations  8.01 us (2%)
    pallas_call x6, Pallas kernels, factor(): pl.pallas_call(factor_kernel, out_shape=(jax.ShapeDtypeStruct((order, ord...  155 us
    dot_general x24, matrix products, dot_tn(): lax.dot_general(a, b, (((0,), (0,)), ((), ())), precision=PRECISE, prefer...  46.6 us
    ppermute x24, starting transfers between devices, shifted(): return lax.ppermute(array, ('tlo', 'thi'), pairs)  40.8 us
    ppermute x24, waiting for transfers between devices, shifted(): return lax.ppermute(array, ('tlo', 'thi'), pairs)  37.1 us
    pallas_call x5, Pallas kernels, solve(): pl.pallas_call(functools.partial(solve_kernel, count), out_shape=tuple((j...  34.1 us
    unnamed x140, local copies, waits for them, and re-layouts  11.9 us
    ppermute x4, waiting for transfers between devices, spread(): lax.ppermute(array, ('tlo', 'thi'), list(zip(holders, others)))  9.95 us
  transfers between devices with their start and end apart: 28, of which 6 were waited for; matrix products, arithmetic and copies ran while one was open for 18% of the time, Pallas kernels for 45%

profile of v3, /device:TPU:0, one launch (start us, length us, event | category | flops | bytes accessed | tf_op | source)
XLA Modules:
  0.0 386.3 jit_solution(1734536314300710068)
XLA Ops:
  2.1 2.4 collective-permute-start
  4.5 29.7 %factor.6 = (f32[512,512]{1,0:T(8,128)S(1)}, f32[512,128]{1,0:T(8,128)S(1)}) custom-call(f32[512,512]{1,0:T(8,128)S(1)} %bitcast.71), custom_call_target="tpu_custom_call" | custom-call | flops 35000000512 | bytes 2097152 | tf_op jit(solution)/shard_map/factor/pallas_call | solution.py:99
  41.0 8.2 %solve.5 = (f32[512,128]{1,0:T(8,128)S(1)}, f32[512,256]{1,0:T(8,128)S(1)}, f32[512,512]{1,0:T(8,128)S(1)}, f32[512,512]{1,0:T(8,128)S(1)}) custom-call(f32[512,512]{1,0:T(8,128)S(1)} %get-tuple-element.57.l_ref, f32[512,128]{1,0:T(8,128)S(1)} %copy-done.55, f32[512,128]{1,0:T(8,128)S(1)} %bitcast.73, f32[512,256]{1,0:T(8,128)S(1)} %bitcast.72, ...), custom_call_target="tpu_custom_call" | custom-call | flops 5000000000 | bytes 8000000 | tf_op jit(solution)/shard_map/solve/pallas_call | solution.py:129
  50.6 1.9 fusion.6
  52.5 1.9 fusion.7
  57.5 2.7 fusion.11
  60.2 2.7 fusion.10
  73.5 29.5 %factor.7 = (f32[512,512]{1,0:T(8,128)S(1)}, f32[512,128]{1,0:T(8,128)S(1)}) custom-call(f32[512,512]{1,0:T(8,128)S(1)} %subtract_subtract_fusion.2.s_ref), custom_call_target="tpu_custom_call" | custom-call | flops 35000000512 | bytes 2097152 | tf_op jit(solution)/shard_map/factor/pallas_call | solution.py:99
  111.5 8.2 %solve.6 = (f32[512,128]{1,0:T(8,128)S(1)}, f32[512,256]{1,0:T(8,128)S(1)}, f32[512,512]{1,0:T(8,128)S(1)}, f32[512,512]{1,0:T(8,128)S(1)}) custom-call(f32[512,512]{1,0:T(8,128)S(1)} %copy-done.14, f32[512,128]{1,0:T(8,128)S(1)} %copy-done.59, f32[512,128]{1,0:T(8,128)S(1)} %slice_subtract_fusion.12.refs_0_, f32[512,256]{1,0:T(8,128)S(1)} %slice_subtract_fusion.5.refs_1_, ...), custom_call_target="tpu_custom_call" | custom-call | flops 5000000000 | bytes 8000000 | tf_op jit(solution)/shard_map/solve/pallas_call | solution.py:129
  121.7 2.8 fusion.18
  124.4 2.3 fusion.13
  131.2 2.7 fusion.17
  133.9 2.8 fusion.16
  136.7 2.8 fusion.15
  139.5 12.1 %collective-permute-done.7 = f32[512,512]{1,0:T(8,128)S(1)} collective-permute-done((f32[512,512]{1,0:T(8,128)S(1)}, f32[512,512]{1,0:T(8,128)S(1)}, u32[]{:S(2)}, u32[]{:S(2)}) %collective-permute-start.7) | collective-permute-done | bytes 1048608 | tf_op jit(solution)/shard_map/ppermute | solution.py:143
  159.1 29.7 %factor.8 = (f32[512,512]{1,0:T(8,128)S(1)}, f32[512,128]{1,0:T(8,128)S(1)}) custom-call(f32[512,512]{1,0:T(8,128)S(1)} %subtract_subtract_fusion.1.s_ref), custom_call_target="tpu_custom_call" | custom-call | flops 35000000512 | bytes 2097152 | tf_op jit(solution)/shard_map/factor/pallas_call | solution.py:99
  197.3 8.2 %solve.7 = (f32[512,128]{1,0:T(8,128)S(1)}, f32[512,256]{1,0:T(8,128)S(1)}, f32[512,512]{1,0:T(8,128)S(1)}, f32[512,512]{1,0:T(8,128)S(1)}) custom-call(f32[512,512]{1,0:T(8,128)S(1)} %copy-done.17, f32[512,128]{1,0:T(8,128)S(1)} %copy-done.57, f32[512,128]{1,0:T(8,128)S(1)} %slice_subtract_fusion.10.refs_0_, f32[512,256]{1,0:T(8,128)S(1)} %slice_subtract_fusion.3.refs_1_, ...), custom_call_target="tpu_custom_call" | custom-call | flops 5000000000 | bytes 8000000 | tf_op jit(solution)/shard_map/solve/pallas_call | solution.py:129
  207.4 1.9 fusion.21
  219.7 22.0 %collective-permute-done.14 = f32[512,512]{1,0:T(8,128)S(1)} collective-permute-done((f32[512,512]{1,0:T(8,128)S(1)}, f32[512,512]{1,0:T(8,128)S(1)}, u32[]{:S(2)}, u32[]{:S(2)}) %collective-permute-start.14) | collective-permute-done | bytes 1048608 | tf_op jit(solution)/shard_map/ppermute | solution.py:143
  246.7 29.9 %factor.9 = (f32[512,512]{1,0:T(8,128)S(1)}, f32[512,128]{1,0:T(8,128)S(1)}) custom-call(f32[512,512]{1,0:T(8,128)S(1)} %subtract_subtract_fusion.s_ref), custom_call_target="tpu_custom_call" | custom-call | flops 35000000512 | bytes 2097152 | tf_op jit(solution)/shard_map/factor/pallas_call | solution.py:99
  277.9 5.9 %solve.8 = (f32[512,128]{1,0:T(8,128)S(1)}, f32[512,256]{1,0:T(8,128)S(1)}, f32[512,512]{1,0:T(8,128)S(1)}) custom-call(f32[512,512]{1,0:T(8,128)S(1)} %get-tuple-element.88.l_ref, f32[512,128]{1,0:T(8,128)S(1)} %get-tuple-element.89.v_ref, f32[512,128]{1,0:T(8,128)S(1)} %slice_subtract_fusion.8.refs_0_, f32[512,256]{1,0:T(8,128)S(1)} %slice_subtract_fusion.1.refs_1_, ...), custom_call_target="tpu_custom_call" | custom-call | flops 5000000000 | bytes 8000000 | tf_op jit(solution)/shard_map/solve/pallas_call | solution.py:129
  283.9 2.9 fusion.26
  286.7 5.1 %collective-permute-start.20 = (f32[512,512]{1,0:T(8,128)}, f32[512,512]{1,0:T(8,128)}, u32[]{:S(2)}, u32[]{:S(2)}) collective-permute-start(f32[512,512]{1,0:T(8,128)} %fusion.26), channel_id=1, source_target_pairs={{0,8},{16,24}} | collective-permute-start | bytes 3145736 | tf_op jit(solution)/shard_map/ppermute | solution.py:143
  297.7 2.7 fusion.27
  300.4 3.0 collective-permute-done.20
  304.9 6.2 %collective-permute-start.23 = (f32[136,384]{1,0:T(8,128)}, f32[136,384]{1,0:T(8,128)}, u32[]{:S(2)}, u32[]{:S(2)}) collective-permute-start(f32[136,384]{1,0:T(8,128)} %get-tuple-element.103), channel_id=1, source_target_pairs={{0,8},{16,24}} | collective-permute-start | bytes 626696 | tf_op jit(solution)/shard_map/ppermute | solution.py:143
  311.1 2.2 collective-permute-start.22
  313.4 29.5 %factor.10 = (f32[512,512]{1,0:T(8,128)S(1)}, f32[512,128]{1,0:T(8,128)S(1)}) custom-call(f32[512,512]{1,0:T(8,128)S(1)} %sub.102.s_ref), custom_call_target="tpu_custom_call" | custom-call | flops 35000000512 | bytes 2097152 | tf_op jit(solution)/shard_map/factor/pallas_call | solution.py:99
  348.2 3.6 solve.9
  356.2 5.9 %collective-permute-done.24 = f32[136,384]{1,0:T(8,128)S(1)} collective-permute-done((f32[136,384]{1,0:T(8,128)S(1)}, f32[136,384]{1,0:T(8,128)S(1)}, u32[]{:S(2)}, u32[]{:S(2)}) %collective-permute-start.24) | collective-permute-done | bytes 208928 | tf_op jit(solution)/shard_map/ppermute | solution.py:151
  369.1 2.2 collective-permute-done.26
  374.6 6.5 %factor.11 = (f32[128,128]{1,0:T(8,128)}, f32[128,128]{1,0:T(8,128)S(1)}) custom-call(f32[128,128]{1,0:T(8,128)S(1)} %slice_subtract_fusion.16.s_ref), custom_call_target="tpu_custom_call" | custom-call | flops 35000000512 | bytes 131072 | tf_op jit(solution)/shard_map/factor/pallas_call | solution.py:99
  (250 shorter events, 98.1 us)
Async XLA Ops:
  2.1 34.3 %collective-permute-start = (f32[512,512]{1,0:T(8,128)S(1)}, f32[512,512]{1,0:T(8,128)S(1)}, u32[]{:S(2)}, u32[]{:S(2)}) collective-permute-start(f32[512,512]{1,0:T(8,128)S(1)} %select_bitcast_fusion.3.refs_2_), channel_id=1, source_target_pairs={{0,1},{2,3},{4,5},{6,7},{8,9},{10,11},{12,13},{14,15},{16,17},{18,... | collective-permute-start | bytes 3145736 | tf_op jit(solution)/shard_map/ppermute | solution.py:143
  54.4 12.3 %collective-permute-start.2 = (f32[512,512]{1,0:T(8,128)S(1)}, f32[512,512]{1,0:T(8,128)S(1)}, u32[]{:S(2)}, u32[]{:S(2)}) collective-permute-start(f32[512,512]{1,0:T(8,128)S(1)} %fusion.7), channel_id=1, source_target_pairs={{1,2},{3,4},{5,6},{7,8},{9,10},{11,12},{13,14},{17,18},{19,20},{21... | collective-permute-start | bytes 3145736 | tf_op jit(solution)/shard_map/ppermute | solution.py:143
  55.5 11.2 %collective-permute-start.1 = (f32[512,512]{1,0:T(8,128)S(1)}, f32[512,512]{1,0:T(8,128)S(1)}, u32[]{:S(2)}, u32[]{:S(2)}) collective-permute-start(f32[512,512]{1,0:T(8,128)S(1)} %fusion.6), channel_id=1, source_target_pairs={{1,0},{3,2},{5,4},{7,6},{9,8},{11,10},{13,12},{15,14},{17,16},{19,... | collective-permute-start | bytes 3145736 | tf_op jit(solution)/shard_map/ppermute | solution.py:143
  67.1 62.4 %collective-permute-start.9 = (f32[136,384]{1,0:T(8,128)}, f32[136,384]{1,0:T(8,128)}, u32[]{:S(2)}, u32[]{:S(2)}) collective-permute-start(f32[136,384]{1,0:T(8,128)} %concatenate.35), channel_id=1, source_target_pairs={{1,0},{3,2},{5,4},{7,6},{9,8},{11,10},{13,12},{15,14},{17,16},{19,... | collective-permute-start | bytes 626696 | tf_op jit(solution)/shard_map/ppermute | solution.py:143
  68.4 37.6 %collective-permute-start.3 = (f32[512,384]{1,0:T(8,128)}, f32[512,384]{1,0:T(8,128)}, u32[]{:S(2)}, u32[]{:S(2)}) collective-permute-start(f32[512,384]{1,0:T(8,128)} %fusion.10), channel_id=1, source_target_pairs={{1,0},{3,2},{5,4},{7,6},{9,8},{11,10},{13,12},{15,14},{17,16},{19,... | collective-permute-start | bytes 2359304 | tf_op jit(solution)/shard_map/ppermute | solution.py:143
  69.7 36.3 %collective-permute-start.4 = (f32[512,384]{1,0:T(8,128)}, f32[512,384]{1,0:T(8,128)}, u32[]{:S(2)}, u32[]{:S(2)}) collective-permute-start(f32[512,384]{1,0:T(8,128)} %fusion.11), channel_id=1, source_target_pairs={{1,2},{3,4},{5,6},{7,8},{9,10},{11,12},{13,14},{17,18},{19,20},{21... | collective-permute-start | bytes 2359304 | tf_op jit(solution)/shard_map/ppermute | solution.py:143
  71.3 37.4 %collective-permute-start.5 = (f32[512,512]{1,0:T(8,128)S(1)}, f32[512,512]{1,0:T(8,128)}, u32[]{:S(2)}, u32[]{:S(2)}) collective-permute-start(f32[512,512]{1,0:T(8,128)S(1)} %fusion.8), channel_id=1, source_target_pairs={{1,0},{3,2},{5,4},{7,6},{9,8},{11,10},{13,12},{15,14},{17,16},{19,... | collective-permute-start | bytes 3145736 | tf_op jit(solution)/shard_map/ppermute | solution.py:143
  72.6 36.0 %collective-permute-start.6 = (f32[512,512]{1,0:T(8,128)S(1)}, f32[512,512]{1,0:T(8,128)S(1)}, u32[]{:S(2)}, u32[]{:S(2)}) collective-permute-start(f32[512,512]{1,0:T(8,128)S(1)} %fusion.9), channel_id=1, source_target_pairs={{1,2},{3,4},{5,6},{7,8},{9,10},{11,12},{13,14},{17,18},{19,20},{21... | collective-permute-start | bytes 3145736 | tf_op jit(solution)/shard_map/ppermute | solution.py:143
  126.7 12.8 %collective-permute-start.8 = (f32[512,512]{1,0:T(8,128)S(1)}, f32[512,512]{1,0:T(8,128)S(1)}, u32[]{:S(2)}, u32[]{:S(2)}) collective-permute-start(f32[512,512]{1,0:T(8,128)S(1)} %fusion.14), channel_id=1, source_target_pairs={{2,4},{6,8},{10,12},{18,20},{22,24},{26,28}} | collective-permute-start | bytes 3145736 | tf_op jit(solution)/shard_map/ppermute | solution.py:143
  127.5 24.1 %collective-permute-start.7 = (f32[512,512]{1,0:T(8,128)S(1)}, f32[512,512]{1,0:T(8,128)S(1)}, u32[]{:S(2)}, u32[]{:S(2)}) collective-permute-start(f32[512,512]{1,0:T(8,128)S(1)} %fusion.13), channel_id=1, source_target_pairs={{2,0},{6,4},{10,8},{14,12},{18,16},{22,20},{26,24},{30,28}} | collective-permute-start | bytes 3145736 | tf_op jit(solution)/shard_map/ppermute | solution.py:143
  152.0 60.4 %collective-permute-start.16 = (f32[136,384]{1,0:T(8,128)}, f32[136,384]{1,0:T(8,128)}, u32[]{:S(2)}, u32[]{:S(2)}) collective-permute-start(f32[136,384]{1,0:T(8,128)} %pad_add_fusion.2), channel_id=1, source_target_pairs={{2,0},{6,4},{10,8},{14,12},{18,16},{22,20},{26,24},{30,28}} | collective-permute-start | bytes 626696 | tf_op jit(solution)/shard_map/ppermute | solution.py:143
  153.3 38.5 %collective-permute-start.10 = (f32[512,384]{1,0:T(8,128)}, f32[512,384]{1,0:T(8,128)}, u32[]{:S(2)}, u32[]{:S(2)}) collective-permute-start(f32[512,384]{1,0:T(8,128)} %fusion.17), channel_id=1, source_target_pairs={{2,0},{6,4},{10,8},{14,12},{18,16},{22,20},{26,24},{30,28}} | collective-permute-start | bytes 2359304 | tf_op jit(solution)/shard_map/ppermute | solution.py:143
  154.6 37.2 %collective-permute-start.11 = (f32[512,384]{1,0:T(8,128)}, f32[512,384]{1,0:T(8,128)}, u32[]{:S(2)}, u32[]{:S(2)}) collective-permute-start(f32[512,384]{1,0:T(8,128)} %fusion.18), channel_id=1, source_target_pairs={{2,4},{6,8},{10,12},{18,20},{22,24},{26,28}} | collective-permute-start | bytes 2359304 | tf_op jit(solution)/shard_map/ppermute | solution.py:143
  156.1 39.6 %collective-permute-start.12 = (f32[512,512]{1,0:T(8,128)}, f32[512,512]{1,0:T(8,128)}, u32[]{:S(2)}, u32[]{:S(2)}) collective-permute-start(f32[512,512]{1,0:T(8,128)} %fusion.15), channel_id=1, source_target_pairs={{2,0},{6,4},{10,8},{14,12},{18,16},{22,20},{26,24},{30,28}} | collective-permute-start | bytes 3145736 | tf_op jit(solution)/shard_map/ppermute | solution.py:143
  157.4 36.9 %collective-permute-start.13 = (f32[512,512]{1,0:T(8,128)}, f32[512,512]{1,0:T(8,128)}, u32[]{:S(2)}, u32[]{:S(2)}) collective-permute-start(f32[512,512]{1,0:T(8,128)} %fusion.16), channel_id=1, source_target_pairs={{2,4},{6,8},{10,12},{18,20},{22,24},{26,28}} | collective-permute-start | bytes 3145736 | tf_op jit(solution)/shard_map/ppermute | solution.py:143
  209.3 10.4 %collective-permute-start.15 = (f32[512,512]{1,0:T(8,128)S(1)}, f32[512,512]{1,0:T(8,128)S(1)}, u32[]{:S(2)}, u32[]{:S(2)}) collective-permute-start(f32[512,512]{1,0:T(8,128)S(1)} %fusion.21), channel_id=1, source_target_pairs={{4,8},{20,24}} | collective-permute-start | bytes 3145736 | tf_op jit(solution)/shard_map/ppermute | solution.py:143
  210.0 31.7 %collective-permute-start.14 = (f32[512,512]{1,0:T(8,128)S(1)}, f32[512,512]{1,0:T(8,128)S(1)}, u32[]{:S(2)}, u32[]{:S(2)}) collective-permute-start(f32[512,512]{1,0:T(8,128)S(1)} %fusion.20), channel_id=1, source_target_pairs={{4,0},{12,8},{20,16},{28,24}} | collective-permute-start | bytes 3145736 | tf_op jit(solution)/shard_map/ppermute | solution.py:143
  242.1 53.8 %collective-permute-start.21 = (f32[136,384]{1,0:T(8,128)}, f32[136,384]{1,0:T(8,128)}, u32[]{:S(2)}, u32[]{:S(2)}) collective-permute-start(f32[136,384]{1,0:T(8,128)} %get-tuple-element.96), channel_id=1, source_target_pairs={{4,0},{12,8},{20,16},{28,24}} | collective-permute-start | bytes 626696 | tf_op jit(solution)/shard_map/ppermute | solution.py:143
  243.4 33.4 %collective-permute-start.17 = (f32[512,384]{1,0:T(8,128)S(1)}, f32[512,384]{1,0:T(8,128)S(1)}, u32[]{:S(2)}, u32[]{:S(2)}) collective-permute-start(f32[512,384]{1,0:T(8,128)S(1)} %fusion.23), channel_id=1, source_target_pairs={{4,0},{12,8},{20,16},{28,24}} | collective-permute-start | bytes 2359304 | tf_op jit(solution)/shard_map/ppermute | solution.py:143
  244.7 32.1 %collective-permute-start.18 = (f32[512,384]{1,0:T(8,128)S(1)}, f32[512,384]{1,0:T(8,128)S(1)}, u32[]{:S(2)}, u32[]{:S(2)}) collective-permute-start(f32[512,384]{1,0:T(8,128)S(1)} %fusion.24), channel_id=1, source_target_pairs={{4,8},{20,24}} | collective-permute-start | bytes 2359304 | tf_op jit(solution)/shard_map/ppermute | solution.py:143
  245.4 31.6 %collective-permute-start.19 = (f32[512,512]{1,0:T(8,128)S(1)}, f32[512,512]{1,0:T(8,128)S(1)}, u32[]{:S(2)}, u32[]{:S(2)}) collective-permute-start(f32[512,512]{1,0:T(8,128)S(1)} %fusion.22), channel_id=1, source_target_pairs={{4,0},{12,8},{20,16},{28,24}} | collective-permute-start | bytes 3145736 | tf_op jit(solution)/shard_map/ppermute | solution.py:143
  286.7 16.7 %collective-permute-start.20 = (f32[512,512]{1,0:T(8,128)}, f32[512,512]{1,0:T(8,128)}, u32[]{:S(2)}, u32[]{:S(2)}) collective-permute-start(f32[512,512]{1,0:T(8,128)} %fusion.26), channel_id=1, source_target_pairs={{0,8},{16,24}} | collective-permute-start | bytes 3145736 | tf_op jit(solution)/shard_map/ppermute | solution.py:143
  304.8 38.0 %copy-start.12 = (f32[512,512]{1,0:T(8,128)S(1)}, f32[512,512]{1,0:T(8,128)}, u32[]{:S(2)}) copy-start(f32[512,512]{1,0:T(8,128)} %copy-done.11) | copy-start | bytes 3145732
  304.8 38.0 %copy-start.15 = (f32[512,512]{1,0:T(8,128)S(1)}, f32[512,512]{1,0:T(8,128)}, u32[]{:S(2)}) copy-start(f32[512,512]{1,0:T(8,128)} %copy-done.13) | copy-start | bytes 3145732
  304.9 38.0 %copy-start.18 = (f32[512,512]{1,0:T(8,128)S(1)}, f32[512,512]{1,0:T(8,128)}, u32[]{:S(2)}) copy-start(f32[512,512]{1,0:T(8,128)} %copy-done.16) | copy-start | bytes 3145732
  304.9 38.0 %copy-start.20 = (f32[512,512]{1,0:T(8,128)S(1)}, f32[512,512]{1,0:T(8,128)}, u32[]{:S(2)}) copy-start(f32[512,512]{1,0:T(8,128)} %copy-done.19) | copy-start | bytes 3145732
  304.9 47.6 %collective-permute-start.23 = (f32[136,384]{1,0:T(8,128)}, f32[136,384]{1,0:T(8,128)}, u32[]{:S(2)}, u32[]{:S(2)}) collective-permute-start(f32[136,384]{1,0:T(8,128)} %get-tuple-element.103), channel_id=1, source_target_pairs={{0,8},{16,24}} | collective-permute-start | bytes 626696 | tf_op jit(solution)/shard_map/ppermute | solution.py:143
  311.1 34.6 %collective-permute-start.22 = (f32[512,384]{1,0:T(8,128)}, f32[512,384]{1,0:T(8,128)}, u32[]{:S(2)}, u32[]{:S(2)}) collective-permute-start(f32[512,384]{1,0:T(8,128)} %fusion.27), channel_id=1, source_target_pairs={{0,8},{16,24}} | collective-permute-start | bytes 2359304 | tf_op jit(solution)/shard_map/ppermute | solution.py:143
  353.5 8.6 %collective-permute-start.24 = (f32[136,384]{1,0:T(8,128)S(1)}, f32[136,384]{1,0:T(8,128)S(1)}, u32[]{:S(2)}, u32[]{:S(2)}) collective-permute-start(f32[136,384]{1,0:T(8,128)S(1)} %add_select_fusion), channel_id=1, source_target_pairs={{8,0},{24,16}} | collective-permute-start | bytes 626696 | tf_op jit(solution)/shard_map/ppermute | solution.py:151
  362.1 4.6 %collective-permute-start.25 = (f32[136,384]{1,0:T(8,128)S(1)}, f32[136,384]{1,0:T(8,128)S(1)}, u32[]{:S(2)}, u32[]{:S(2)}) collective-permute-start(f32[136,384]{1,0:T(8,128)S(1)} %add.110), channel_id=1, source_target_pairs={{8,12},{0,4},{24,28},{16,20}} | collective-permute-start | bytes 626696 | tf_op jit(solution)/shard_map/ppermute | solution.py:151
  366.8 4.6 %collective-permute-start.26 = (f32[136,384]{1,0:T(8,128)S(1)}, f32[136,384]{1,0:T(8,128)S(1)}, u32[]{:S(2)}, u32[]{:S(2)}) collective-permute-start(f32[136,384]{1,0:T(8,128)S(1)} %add.111), channel_id=1, source_target_pairs={{8,10},{0,2},{12,14},{4,6},{24,26},{16,18},{28,30},{20,22}} | collective-permute-start | bytes 626696 | tf_op jit(solution)/shard_map/ppermute | solution.py:151
  371.4 2.4 collective-permute-start.27
  (64 other events, 347.6 us)
